TPU v7x, 256 devices: a whole 4x4x8 slice. The times are simulated.
256 devices in a mesh: gx: 4 (over y_hi, core), yz: 64 (over y_lo, z, x).
Axes of the slice: x: 4, y: 4 (y_hi: 2, y_lo: 2; y = y_hi * 2 + y_lo), z: 8, core: 2. Of those that a mesh axis runs over, the one named last changes fastest.
Arguments:
- terminal_adjoint: float32 [4, 32, 64, 64, 128], P(None, 'gx', None, 'yz'), may hold values from -6 to 6
- diffusivity: float32 [4, 32, 64, 64, 128], P(None, 'gx', None, 'yz'), may hold values from 0.02 to 0.08
- velocity: float32 [3, 32, 64, 64, 128], P(None, 'gx', None, 'yz'), may hold values from -1 to 1
- charge_modes: float32 [32, 64, 16, 512], P('gx', 'yz'), may hold values from -0.6 to 0.6
Outputs:
- adjoint: float32 [4, 32, 64, 64, 128], P(None, 'gx', None, 'yz')
All inputs are finite; a program needn't handle non-finite values.
Results may differ from a plain program's by a relative error of at most 0.00005.
Values sent between devices are 32-bit elements; how exact they have to be, the bound alone decides.
A program may use at most 64 MiB of HBM per device.

v0:
```python
import math

import jax
import jax.numpy as jnp
from jax import lax
from jax.sharding import PartitionSpec as P

SPECIES = 4
STEPS = 3


VALENCE = (1.0, -1.0, 2.0, -1.0)
SCREEN = 1.0


def extended(block, sides, width):
    for axis, dim in sides:
        count = lax.axis_size(axis)
        forward = [(i, i + 1) for i in range(count - 1)]
        backward = [(target, source) for source, target in forward]
        low = lax.ppermute(
            lax.slice_in_dim(block, block.shape[dim] - width, None, axis=dim), axis, forward
        )
        high = lax.ppermute(lax.slice_in_dim(block, 0, width, axis=dim), axis, backward)
        block = jnp.concatenate([low, block, high], axis=dim)
    return block


def from_behind(block, axis, distance):
    devices = range(lax.axis_size(axis))
    route = [(i - distance, i) for i in devices if i - distance in devices]
    return lax.ppermute(block, axis, route)


def column_table(length):
    half = length // 2
    modes = lax.iota(jnp.int32, half)[:, None]
    cells = lax.iota(jnp.int32, length)[None, :]
    phase = (modes * cells % length).astype(jnp.float32)
    angle = phase * (2.0 * math.pi / length)
    theta = modes.astype(jnp.float32) * (2.0 * math.pi / length)
    green = 1.0 / (1.0 + SCREEN * theta * theta)
    return jnp.concatenate([jnp.cos(angle) * green, jnp.sin(angle) * green], 0)


def faces(field, widened, row_low, row_high, below, above, low_ok, high_ok):
    x_plus = widened[:, 2:]
    x_minus = widened[:, :-2]
    y_plus = jnp.concatenate([field[:, :, 1:], row_high[:, :, None] * high_ok], 2)
    y_minus = jnp.concatenate([row_low[:, :, None] * low_ok, field[:, :, :-1]], 2)
    z_plus = jnp.concatenate([field[..., 1:], above[..., None]], 4)
    z_minus = jnp.concatenate([below[..., None], field[..., :-1]], 4)
    return (x_plus, x_minus, y_plus, y_minus, z_plus, z_minus)


def rims(field, low_ok, high_ok, blocks_y):
    widened = extended(field, (("gx", 1),), 1)
    row_low = from_behind(field[:, :, -1], "yz", 1)
    row_high = from_behind(field[:, :, 0], "yz", -1)
    below = from_behind(field[..., -1], "yz", blocks_y)
    above = from_behind(field[..., 0], "yz", -blocks_y)
    return faces(field, widened, row_low, row_high, below, above, low_ok, high_ok)


def advance(adjoint, near, diffusion, velocity, slopes, valence):
    x_plus, x_minus, y_plus, y_minus, z_plus, z_minus = near
    spread = x_plus + x_minus + (y_plus + y_minus) + (z_plus + z_minus) - 6.0 * adjoint
    drift = 0.25 * valence * diffusion
    change = diffusion * spread
    change = change + (0.5 * velocity[0] - drift * slopes[0]) * (x_plus - x_minus)
    change = change + (0.5 * velocity[1] - drift * slopes[1]) * (y_plus - y_minus)
    change = change + (0.5 * velocity[2] - drift * slopes[2]) * (z_plus - z_minus)
    return adjoint + change


def body(terminal_adjoint, diffusivity, velocity, charge_modes):
    slab, rows_dev, blocks_y, length = charge_modes.shape
    depth = terminal_adjoint.shape[4]
    layers = length // depth
    table = column_table(length).reshape(length, layers, depth)
    pencil = jnp.einsum(
        "xrpk,kjb->xrjpb",
        charge_modes,
        table,
        precision=lax.Precision.HIGHEST,
        preferred_element_type=jnp.float32,
    )
    pencil = pencil.reshape(slab, rows_dev, layers * blocks_y, depth)
    potential = lax.all_to_all(pencil, "yz", split_axis=2, concat_axis=1, tiled=True)[None]
    position = lax.axis_index("yz") % blocks_y
    low_ok = (position > 0).astype(jnp.float32)
    high_ok = (position < blocks_y - 1).astype(jnp.float32)
    valence = jnp.array(VALENCE, jnp.float32).reshape(SPECIES, 1, 1, 1, 1)
    adjoint = terminal_adjoint
    for repeat in range(STEPS):
        joined = rims(jnp.concatenate([adjoint, potential], 0), low_ok, high_ok, blocks_y)
        near = tuple((piece[:-1] for piece in joined))
        slopes = (
            joined[0][-1:] - joined[1][-1:],
            joined[2][-1:] - joined[3][-1:],
            joined[4][-1:] - joined[5][-1:],
        )
        adjoint = advance(adjoint, near, diffusivity, velocity, slopes, valence)
    return adjoint


def solution(mesh):
    return jax.shard_map(
        body,
        mesh=mesh,
        in_specs=(
            P(None, "gx", None, "yz", None),
            P(None, "gx", None, "yz", None),
            P(None, "gx", None, "yz", None),
            P("gx", "yz", None, None),
        ),
        out_specs=P(None, "gx", None, "yz", None),
        check_vma=False,
    )
```

profile of v0, /device:TPU:9, one launch (start us, length us, event | category | flops | bytes accessed | tf_op | source)
XLA Modules:
  0.0 172.7 jit_solution(12766363783160037561)
XLA Ops:
  3.7 12.5 %all-to-all-start = ((f32[8,1,64,128]{3,0,1,2:T(8,128)}), f32[8,1,64,128]{3,0,1,2:T(8,128)S(1)}, u32[]{:S(2)}, u32[]{:S(2)}) async-start(f32[8,1,64,128]{3,0,1,2:T(8,128)} %copy.315), calls=%async_computation | async-start | bytes 524288 | tf_op jit(solution)/shard_map/all_to_all | solution.py:89
  20.0 6.0 %all-to-all-done = f32[8,1,64,128]{3,0,1,2:T(8,128)S(1)} async-done(((f32[8,1,64,128]{3,0,1,2:T(8,128)}), f32[8,1,64,128]{3,0,1,2:T(8,128)S(1)}, u32[]{:S(2)}, u32[]{:S(2)}) %all-to-all-start) | async-done | bytes 262176 | tf_op jit(solution)/shard_map/all_to_all | solution.py:89
  30.9 2.4 %copy.319 = f32[5,8,64,1,1]{2,1,0,4,3:T(8,128)} copy(f32[5,8,64,1,1]{4,1,0,3,2:T(8,128)} %get-tuple-element.33) | data formatting | bytes 20480 | tf_op jit(solution)/shard_map/slice | solution.py:60
  35.1 6.3 %collective-permute-start.4 = (f32[5,8,64,1]{2,1,0,3:T(8,128)S(1)}, f32[5,8,64,1]{2,1,0,3:T(8,128)}, u32[]{:S(2)}, u32[]{:S(2)}) collective-permute-start(f32[5,8,64,1]{2,1,0,3:T(8,128)S(1)} %bitcast.100), channel_id=1, source_target_pairs={{16,0},{17,1},{18,2},{19,3},{20,4},{21,5},{22,6},{23,7},{24,8},{25... | collective-permute-start | bytes 30728 | tf_op jit(solution)/shard_map/ppermute | solution.py:32
  41.4 3.4 %collective-permute-start.5 = (f32[5,8,64,1]{2,1,0,3:T(8,128)}, f32[5,8,64,1]{2,1,0,3:T(8,128)}, u32[]{:S(2)}, u32[]{:S(2)}) collective-permute-start(f32[5,8,64,1]{2,1,0,3:T(8,128)} %bitcast.14), channel_id=1, source_target_pairs={{0,16},{1,17},{2,18},{3,19},{4,20},{5,21},{6,22},{7,23},{8,24},{9,... | collective-permute-start | bytes 30728 | tf_op jit(solution)/shard_map/ppermute | solution.py:32
  44.9 2.3 %collective-permute-start.3 = (f32[5,8,1,128]{3,1,0,2:T(8,128)S(1)}, f32[5,8,1,128]{3,1,0,2:T(8,128)S(1)}, u32[]{:S(2)}, u32[]{:S(2)}) collective-permute-start(f32[5,8,1,128]{3,1,0,2:T(8,128)S(1)} %get-tuple-element.5), channel_id=1, source_target_pairs={{0,1},{1,2},{2,3},{3,4},{4,5},{5,6},{6,7},{7,8},{8,9},{9,10},{10,1... | collective-permute-start | bytes 61448 | tf_op jit(solution)/shard_map/ppermute | solution.py:32
  47.2 7.2 %collective-permute-start.2 = (f32[5,8,1,128]{3,1,0,2:T(8,128)S(1)}, f32[5,8,1,128]{3,1,0,2:T(8,128)S(1)}, u32[]{:S(2)}, u32[]{:S(2)}) collective-permute-start(f32[5,8,1,128]{3,1,0,2:T(8,128)S(1)} %get-tuple-element.29), channel_id=1, source_target_pairs={{1,0},{2,1},{3,2},{4,3},{5,4},{6,5},{7,6},{8,7},{9,8},{10,9},{11,1... | collective-permute-start | bytes 61448 | tf_op jit(solution)/shard_map/ppermute | solution.py:32
  54.4 6.5 %collective-permute-start = (f32[5,1,64,1,128]{4,1,0,3,2:T(1,128)}, f32[5,1,64,1,128]{4,1,0,3,2:T(1,128)}, u32[]{:S(2)}, u32[]{:S(2)}) collective-permute-start(f32[5,1,64,1,128]{4,1,0,3,2:T(1,128)} %get-tuple-element.27), channel_id=1, source_target_pairs={{64,0},{128,64},{192,128},{65,1},{129,65},{193,129},{66,2},{130,66... | collective-permute-start | bytes 491528 | tf_op jit(solution)/shard_map/ppermute | solution.py:24
  60.9 4.0 %collective-permute-start.1 = (f32[5,1,64,1,128]{4,1,0,3,2:T(1,128)}, f32[5,1,64,1,128]{4,1,0,3,2:T(1,128)}, u32[]{:S(2)}, u32[]{:S(2)}) collective-permute-start(f32[5,1,64,1,128]{4,1,0,3,2:T(1,128)} %get-tuple-element.28), channel_id=1, source_target_pairs={{0,64},{64,128},{128,192},{1,65},{65,129},{129,193},{2,66},{66,130... | collective-permute-start | bytes 491528 | tf_op jit(solution)/shard_map/ppermute | solution.py:21
  64.9 2.3 %copy.320 = f32[5,8,64,1,1]{4,1,0,3,2:T(8,128)} copy(f32[5,8,64,1,1]{2,1,0,4,3:T(8,128)} %bitcast.15) | data formatting | bytes 20480 | tf_op jit(solution)/shard_map/broadcast_in_dim | solution.py:52
  67.2 2.3 %copy.318 = f32[5,8,64,1,1]{4,1,0,3,2:T(8,128)} copy(f32[5,8,64,1,1]{2,1,0,4,3:T(8,128)} %bitcast.13) | data formatting | bytes 20480 | tf_op jit(solution)/shard_map/broadcast_in_dim | solution.py:51
  75.5 2.7 %fusion.40 = f32[4,8,64,1,128]{4,1,0,3,2:T(8,128)S(1)} fusion(f32[5,8,64,1,1]{4,1,0,3,2:T(8,128)S(1)} %copy-done.5, f32[5,8,64,1,127]{4,1,0,3,2:T(8,128)S(1)} %copy-done.3, f32[5,8,64,1,128]{4,1,0,3,2:T(8,128)S(1)} %fusion.15, f32[5,8,1,1,128]{4,1,0,3,2:T(8,128)S(1)} %multiply_bitcast_fusion.5, f32[5,8,63,1,128]{4,1,0,3,2:T(8,128)S(1)} %copy-done.15, ...), kind=kLoop, calls=%fused_computation.111 | loop fusion | flops 7340032 | bytes 11796496 | tf_op jit(solution)/shard_map/add | solution.py:73
  86.8 4.2 %collective-permute-start.10 = (f32[5,8,64,1]{2,1,0,3:T(8,128)S(1)}, f32[5,8,64,1]{2,1,0,3:T(8,128)S(1)}, u32[]{:S(2)}, u32[]{:S(2)}) collective-permute-start(f32[5,8,64,1]{2,1,0,3:T(8,128)S(1)} %bitcast.98), channel_id=1, source_target_pairs={{16,0},{17,1},{18,2},{19,3},{20,4},{21,5},{22,6},{23,7},{24,8},{25... | collective-permute-start | bytes 30728 | tf_op jit(solution)/shard_map/ppermute | solution.py:32
  90.9 5.0 %collective-permute-start.11 = (f32[5,8,64,1]{2,1,0,3:T(8,128)S(1)}, f32[5,8,64,1]{2,1,0,3:T(8,128)S(1)}, u32[]{:S(2)}, u32[]{:S(2)}) collective-permute-start(f32[5,8,64,1]{2,1,0,3:T(8,128)S(1)} %bitcast.103), channel_id=1, source_target_pairs={{0,16},{1,17},{2,18},{3,19},{4,20},{5,21},{6,22},{7,23},{8,24},{9,... | collective-permute-start | bytes 30728 | tf_op jit(solution)/shard_map/ppermute | solution.py:32
  98.1 7.6 %collective-permute-start.8 = (f32[5,8,1,128]{3,1,0,2:T(8,128)S(1)}, f32[5,8,1,128]{3,1,0,2:T(8,128)S(1)}, u32[]{:S(2)}, u32[]{:S(2)}) collective-permute-start(f32[5,8,1,128]{3,1,0,2:T(8,128)S(1)} %get-tuple-element.38), channel_id=1, source_target_pairs={{1,0},{2,1},{3,2},{4,3},{5,4},{6,5},{7,6},{8,7},{9,8},{10,9},{11,1... | collective-permute-start | bytes 61448 | tf_op jit(solution)/shard_map/ppermute | solution.py:32
  105.7 2.1 %collective-permute-start.6 = (f32[5,1,64,1,128]{4,1,0,3,2:T(1,128)S(1)}, f32[5,1,64,1,128]{4,1,0,3,2:T(1,128)S(1)}, u32[]{:S(2)}, u32[]{:S(2)}) collective-permute-start(f32[5,1,64,1,128]{4,1,0,3,2:T(1,128)S(1)} %get-tuple-element.19), channel_id=1, source_target_pairs={{64,0},{128,64},{192,128},{65,1},{129,65},{193,129},{66,2},{130,66... | collective-permute-start | bytes 491528 | tf_op jit(solution)/shard_map/ppermute | solution.py:24
  107.8 5.0 %collective-permute-start.7 = (f32[5,1,64,1,128]{4,1,0,3,2:T(1,128)S(1)}, f32[5,1,64,1,128]{4,1,0,3,2:T(1,128)S(1)}, u32[]{:S(2)}, u32[]{:S(2)}) collective-permute-start(f32[5,1,64,1,128]{4,1,0,3,2:T(1,128)S(1)} %get-tuple-element.20), channel_id=1, source_target_pairs={{0,64},{64,128},{128,192},{1,65},{65,129},{129,193},{2,66},{66,130... | collective-permute-start | bytes 491528 | tf_op jit(solution)/shard_map/ppermute | solution.py:21
  121.4 2.4 %add_add_fusion.1 = f32[4,8,64,1,128]{4,1,0,3,2:T(8,128)S(1)} fusion(f32[4,8,64,1,128]{4,1,0,3,2:T(8,128)S(1)} %fusion.40, f32[5,8,64,1,1]{4,1,0,3,2:T(8,128)S(1)} %copy-done.6, f32[5,8,64,1,127]{4,1,0,3,2:T(8,128)S(1)} %copy-done.1, f32[5,8,64,1,128]{4,1,0,3,2:T(8,128)S(1)} %fusion.16, f32[5,8,1,1,128]{4,1,0,3,2:T(8,128)S(1)} %multiply_bitcast_fusion.3, ...), kind=kLoop, calls=%fused_computation.101 | loop fusion | flops 7340032 | bytes 11796496 | tf_op jit(solution)/shard_map/add | solution.py:73
  131.3 4.2 %collective-permute-start.16 = (f32[5,8,64,1]{2,1,0,3:T(8,128)S(1)}, f32[5,8,64,1]{2,1,0,3:T(8,128)S(1)}, u32[]{:S(2)}, u32[]{:S(2)}) collective-permute-start(f32[5,8,64,1]{2,1,0,3:T(8,128)S(1)} %bitcast.101), channel_id=1, source_target_pairs={{16,0},{17,1},{18,2},{19,3},{20,4},{21,5},{22,6},{23,7},{24,8},{25... | collective-permute-start | bytes 30728 | tf_op jit(solution)/shard_map/ppermute | solution.py:32
  135.5 5.0 %collective-permute-start.17 = (f32[5,8,64,1]{2,1,0,3:T(8,128)S(1)}, f32[5,8,64,1]{2,1,0,3:T(8,128)S(1)}, u32[]{:S(2)}, u32[]{:S(2)}) collective-permute-start(f32[5,8,64,1]{2,1,0,3:T(8,128)S(1)} %bitcast.105), channel_id=1, source_target_pairs={{0,16},{1,17},{2,18},{3,19},{4,20},{5,21},{6,22},{7,23},{8,24},{9,... | collective-permute-start | bytes 30728 | tf_op jit(solution)/shard_map/ppermute | solution.py:32
  143.3 7.6 %collective-permute-start.14 = (f32[5,8,1,128]{3,1,0,2:T(8,128)S(1)}, f32[5,8,1,128]{3,1,0,2:T(8,128)S(1)}, u32[]{:S(2)}, u32[]{:S(2)}) collective-permute-start(f32[5,8,1,128]{3,1,0,2:T(8,128)S(1)} %get-tuple-element.36), channel_id=1, source_target_pairs={{1,0},{2,1},{3,2},{4,3},{5,4},{6,5},{7,6},{8,7},{9,8},{10,9},{11,1... | collective-permute-start | bytes 61448 | tf_op jit(solution)/shard_map/ppermute | solution.py:32
  153.4 5.4 %collective-permute-start.13 = (f32[5,1,64,1,128]{4,1,0,3,2:T(1,128)}, f32[5,1,64,1,128]{4,1,0,3,2:T(1,128)}, u32[]{:S(2)}, u32[]{:S(2)}) collective-permute-start(f32[5,1,64,1,128]{4,1,0,3,2:T(1,128)} %get-tuple-element.12), channel_id=1, source_target_pairs={{0,64},{64,128},{128,192},{1,65},{65,129},{129,193},{2,66},{66,130... | collective-permute-start | bytes 491528 | tf_op jit(solution)/shard_map/ppermute | solution.py:21
  158.8 2.3 %copy.336 = f32[5,8,64,1,1]{4,1,0,3,2:T(8,128)} copy(f32[5,8,64,1,1]{2,1,0,4,3:T(8,128)} %bitcast.106) | data formatting | bytes 20480 | tf_op jit(solution)/shard_map/broadcast_in_dim | solution.py:52
  168.2 2.4 %add_add_fusion = f32[4,8,64,1,128]{4,1,0,3,2:T(8,128)S(1)} fusion(f32[4,8,64,1,128]{4,1,0,3,2:T(8,128)S(1)} %add_add_fusion.1, f32[5,8,64,1,1]{4,1,0,3,2:T(8,128)S(1)} %copy-done.4, f32[5,8,64,1,127]{4,1,0,3,2:T(8,128)S(1)} %fusion.7, f32[5,8,64,1,128]{4,1,0,3,2:T(8,128)S(1)} %fusion.17, f32[5,8,1,1,128]{4,1,0,3,2:T(8,128)S(1)} %multiply_bitcast_fusion.1, ...), kind=kLoop, calls=%fused_computation.100 | loop fusion | flops 7340032 | bytes 11796496 | tf_op jit(solution)/shard_map/add | solution.py:73
  (127 shorter events, 61.1 us)
Async XLA Ops:
  0.0 2.1 %copy-start = (f32[8,1,16,512]{3,2,1,0:T(8,128)S(1)}, f32[8,1,16,512]{3,2,1,0:T(8,128)}, u32[]{:S(2)}) copy-start(f32[8,1,16,512]{3,2,1,0:T(8,128)} %param.8) | copy-start | bytes 786436
  3.7 22.3 %all-to-all-start = ((f32[8,1,64,128]{3,0,1,2:T(8,128)}), f32[8,1,64,128]{3,0,1,2:T(8,128)S(1)}, u32[]{:S(2)}, u32[]{:S(2)}) async-start(f32[8,1,64,128]{3,0,1,2:T(8,128)} %copy.315), calls=%async_computation | async-start | bytes 524288 | tf_op jit(solution)/shard_map/all_to_all | solution.py:89
  16.2 3.2 %copy-start.21 = (f32[4,8,64,1,128]{4,3,2,1,0:T(1,128)S(1)}, f32[4,8,64,1,128]{4,3,2,1,0:T(1,128)}, u32[]{:S(2)}) copy-start(f32[4,8,64,1,128]{4,3,2,1,0:T(1,128)} %param.5) | copy-start | bytes 3145732
  27.3 44.0 %copy-start.2 = (f32[5,8,64,1,127]{4,1,0,3,2:T(8,128)}, f32[5,8,64,1,127]{4,1,0,3,2:T(8,128)S(1)}, u32[]{:S(2)}) copy-start(f32[5,8,64,1,127]{4,1,0,3,2:T(8,128)S(1)} %fusion.13) | copy-start | bytes 3901444
  35.1 32.1 %collective-permute-start.4 = (f32[5,8,64,1]{2,1,0,3:T(8,128)S(1)}, f32[5,8,64,1]{2,1,0,3:T(8,128)}, u32[]{:S(2)}, u32[]{:S(2)}) collective-permute-start(f32[5,8,64,1]{2,1,0,3:T(8,128)S(1)} %bitcast.100), channel_id=1, source_target_pairs={{16,0},{17,1},{18,2},{19,3},{20,4},{21,5},{22,6},{23,7},{24,8},{25... | collective-permute-start | bytes 30728 | tf_op jit(solution)/shard_map/ppermute | solution.py:32
  41.4 19.5 %collective-permute-start.5 = (f32[5,8,64,1]{2,1,0,3:T(8,128)}, f32[5,8,64,1]{2,1,0,3:T(8,128)}, u32[]{:S(2)}, u32[]{:S(2)}) collective-permute-start(f32[5,8,64,1]{2,1,0,3:T(8,128)} %bitcast.14), channel_id=1, source_target_pairs={{0,16},{1,17},{2,18},{3,19},{4,20},{5,21},{6,22},{7,23},{8,24},{9,... | collective-permute-start | bytes 30728 | tf_op jit(solution)/shard_map/ppermute | solution.py:32
  44.9 26.9 %collective-permute-start.3 = (f32[5,8,1,128]{3,1,0,2:T(8,128)S(1)}, f32[5,8,1,128]{3,1,0,2:T(8,128)S(1)}, u32[]{:S(2)}, u32[]{:S(2)}) collective-permute-start(f32[5,8,1,128]{3,1,0,2:T(8,128)S(1)} %get-tuple-element.5), channel_id=1, source_target_pairs={{0,1},{1,2},{2,3},{3,4},{4,5},{5,6},{6,7},{7,8},{8,9},{9,10},{10,1... | collective-permute-start | bytes 61448 | tf_op jit(solution)/shard_map/ppermute | solution.py:32
  47.2 24.6 %collective-permute-start.2 = (f32[5,8,1,128]{3,1,0,2:T(8,128)S(1)}, f32[5,8,1,128]{3,1,0,2:T(8,128)S(1)}, u32[]{:S(2)}, u32[]{:S(2)}) collective-permute-start(f32[5,8,1,128]{3,1,0,2:T(8,128)S(1)} %get-tuple-element.29), channel_id=1, source_target_pairs={{1,0},{2,1},{3,2},{4,3},{5,4},{6,5},{7,6},{8,7},{9,8},{10,9},{11,1... | collective-permute-start | bytes 61448 | tf_op jit(solution)/shard_map/ppermute | solution.py:32
  54.4 18.9 %collective-permute-start = (f32[5,1,64,1,128]{4,1,0,3,2:T(1,128)}, f32[5,1,64,1,128]{4,1,0,3,2:T(1,128)}, u32[]{:S(2)}, u32[]{:S(2)}) collective-permute-start(f32[5,1,64,1,128]{4,1,0,3,2:T(1,128)} %get-tuple-element.27), channel_id=1, source_target_pairs={{64,0},{128,64},{192,128},{65,1},{129,65},{193,129},{66,2},{130,66... | collective-permute-start | bytes 491528 | tf_op jit(solution)/shard_map/ppermute | solution.py:24
  60.9 12.4 %collective-permute-start.1 = (f32[5,1,64,1,128]{4,1,0,3,2:T(1,128)}, f32[5,1,64,1,128]{4,1,0,3,2:T(1,128)}, u32[]{:S(2)}, u32[]{:S(2)}) collective-permute-start(f32[5,1,64,1,128]{4,1,0,3,2:T(1,128)} %get-tuple-element.28), channel_id=1, source_target_pairs={{0,64},{64,128},{128,192},{1,65},{65,129},{129,193},{2,66},{66,130... | collective-permute-start | bytes 491528 | tf_op jit(solution)/shard_map/ppermute | solution.py:21
  73.3 2.1 %copy-start.22 = (f32[4,8,64,1,128]{4,3,2,1,0:T(1,128)S(1)}, f32[4,8,64,1,128]{4,3,2,1,0:T(1,128)}, u32[]{:S(2)}) copy-start(f32[4,8,64,1,128]{4,3,2,1,0:T(1,128)} %param.5) | copy-start | bytes 3145732
  86.8 27.6 %collective-permute-start.10 = (f32[5,8,64,1]{2,1,0,3:T(8,128)S(1)}, f32[5,8,64,1]{2,1,0,3:T(8,128)S(1)}, u32[]{:S(2)}, u32[]{:S(2)}) collective-permute-start(f32[5,8,64,1]{2,1,0,3:T(8,128)S(1)} %bitcast.98), channel_id=1, source_target_pairs={{16,0},{17,1},{18,2},{19,3},{20,4},{21,5},{22,6},{23,7},{24,8},{25... | collective-permute-start | bytes 30728 | tf_op jit(solution)/shard_map/ppermute | solution.py:32
  90.9 16.9 %collective-permute-start.11 = (f32[5,8,64,1]{2,1,0,3:T(8,128)S(1)}, f32[5,8,64,1]{2,1,0,3:T(8,128)S(1)}, u32[]{:S(2)}, u32[]{:S(2)}) collective-permute-start(f32[5,8,64,1]{2,1,0,3:T(8,128)S(1)} %bitcast.103), channel_id=1, source_target_pairs={{0,16},{1,17},{2,18},{3,19},{4,20},{5,21},{6,22},{7,23},{8,24},{9,... | collective-permute-start | bytes 30728 | tf_op jit(solution)/shard_map/ppermute | solution.py:32
  96.2 22.4 %collective-permute-start.9 = (f32[5,8,1,128]{3,1,0,2:T(8,128)S(1)}, f32[5,8,1,128]{3,1,0,2:T(8,128)S(1)}, u32[]{:S(2)}, u32[]{:S(2)}) collective-permute-start(f32[5,8,1,128]{3,1,0,2:T(8,128)S(1)} %get-tuple-element.37), channel_id=1, source_target_pairs={{0,1},{1,2},{2,3},{3,4},{4,5},{5,6},{6,7},{7,8},{8,9},{9,10},{10,1... | collective-permute-start | bytes 61448 | tf_op jit(solution)/shard_map/ppermute | solution.py:32
  98.1 20.5 %collective-permute-start.8 = (f32[5,8,1,128]{3,1,0,2:T(8,128)S(1)}, f32[5,8,1,128]{3,1,0,2:T(8,128)S(1)}, u32[]{:S(2)}, u32[]{:S(2)}) collective-permute-start(f32[5,8,1,128]{3,1,0,2:T(8,128)S(1)} %get-tuple-element.38), channel_id=1, source_target_pairs={{1,0},{2,1},{3,2},{4,3},{5,4},{6,5},{7,6},{8,7},{9,8},{10,9},{11,1... | collective-permute-start | bytes 61448 | tf_op jit(solution)/shard_map/ppermute | solution.py:32
  105.7 14.4 %collective-permute-start.6 = (f32[5,1,64,1,128]{4,1,0,3,2:T(1,128)S(1)}, f32[5,1,64,1,128]{4,1,0,3,2:T(1,128)S(1)}, u32[]{:S(2)}, u32[]{:S(2)}) collective-permute-start(f32[5,1,64,1,128]{4,1,0,3,2:T(1,128)S(1)} %get-tuple-element.19), channel_id=1, source_target_pairs={{64,0},{128,64},{192,128},{65,1},{129,65},{193,129},{66,2},{130,66... | collective-permute-start | bytes 491528 | tf_op jit(solution)/shard_map/ppermute | solution.py:24
  107.8 12.3 %collective-permute-start.7 = (f32[5,1,64,1,128]{4,1,0,3,2:T(1,128)S(1)}, f32[5,1,64,1,128]{4,1,0,3,2:T(1,128)S(1)}, u32[]{:S(2)}, u32[]{:S(2)}) collective-permute-start(f32[5,1,64,1,128]{4,1,0,3,2:T(1,128)S(1)} %get-tuple-element.20), channel_id=1, source_target_pairs={{0,64},{64,128},{128,192},{1,65},{65,129},{129,193},{2,66},{66,130... | collective-permute-start | bytes 491528 | tf_op jit(solution)/shard_map/ppermute | solution.py:21
  115.9 2.5 %copy-start.8 = (f32[5,8,64,1,1]{4,1,0,3,2:T(8,128)S(1)}, f32[5,8,64,1,1]{4,1,0,3,2:T(8,128)}, u32[]{:S(2)}) copy-start(f32[5,8,64,1,1]{4,1,0,3,2:T(8,128)} %copy.331) | copy-start | bytes 30724
  131.3 29.8 %collective-permute-start.16 = (f32[5,8,64,1]{2,1,0,3:T(8,128)S(1)}, f32[5,8,64,1]{2,1,0,3:T(8,128)S(1)}, u32[]{:S(2)}, u32[]{:S(2)}) collective-permute-start(f32[5,8,64,1]{2,1,0,3:T(8,128)S(1)} %bitcast.101), channel_id=1, source_target_pairs={{16,0},{17,1},{18,2},{19,3},{20,4},{21,5},{22,6},{23,7},{24,8},{25... | collective-permute-start | bytes 30728 | tf_op jit(solution)/shard_map/ppermute | solution.py:32
  135.5 17.4 %collective-permute-start.17 = (f32[5,8,64,1]{2,1,0,3:T(8,128)S(1)}, f32[5,8,64,1]{2,1,0,3:T(8,128)S(1)}, u32[]{:S(2)}, u32[]{:S(2)}) collective-permute-start(f32[5,8,64,1]{2,1,0,3:T(8,128)S(1)} %bitcast.105), channel_id=1, source_target_pairs={{0,16},{1,17},{2,18},{3,19},{4,20},{5,21},{6,22},{7,23},{8,24},{9,... | collective-permute-start | bytes 30728 | tf_op jit(solution)/shard_map/ppermute | solution.py:32
  141.4 23.6 %collective-permute-start.15 = (f32[5,8,1,128]{3,1,0,2:T(8,128)S(1)}, f32[5,8,1,128]{3,1,0,2:T(8,128)S(1)}, u32[]{:S(2)}, u32[]{:S(2)}) collective-permute-start(f32[5,8,1,128]{3,1,0,2:T(8,128)S(1)} %get-tuple-element.35), channel_id=1, source_target_pairs={{0,1},{1,2},{2,3},{3,4},{4,5},{5,6},{6,7},{7,8},{8,9},{9,10},{10,1... | collective-permute-start | bytes 61448 | tf_op jit(solution)/shard_map/ppermute | solution.py:32
  143.3 21.7 %collective-permute-start.14 = (f32[5,8,1,128]{3,1,0,2:T(8,128)S(1)}, f32[5,8,1,128]{3,1,0,2:T(8,128)S(1)}, u32[]{:S(2)}, u32[]{:S(2)}) collective-permute-start(f32[5,8,1,128]{3,1,0,2:T(8,128)S(1)} %get-tuple-element.36), channel_id=1, source_target_pairs={{1,0},{2,1},{3,2},{4,3},{5,4},{6,5},{7,6},{8,7},{9,8},{10,9},{11,1... | collective-permute-start | bytes 61448 | tf_op jit(solution)/shard_map/ppermute | solution.py:32
  150.9 15.6 %collective-permute-start.12 = (f32[5,1,64,1,128]{4,1,0,3,2:T(1,128)}, f32[5,1,64,1,128]{4,1,0,3,2:T(1,128)}, u32[]{:S(2)}, u32[]{:S(2)}) collective-permute-start(f32[5,1,64,1,128]{4,1,0,3,2:T(1,128)} %get-tuple-element.11), channel_id=1, source_target_pairs={{64,0},{128,64},{192,128},{65,1},{129,65},{193,129},{66,2},{130,66... | collective-permute-start | bytes 491528 | tf_op jit(solution)/shard_map/ppermute | solution.py:24
  153.4 13.1 %collective-permute-start.13 = (f32[5,1,64,1,128]{4,1,0,3,2:T(1,128)}, f32[5,1,64,1,128]{4,1,0,3,2:T(1,128)}, u32[]{:S(2)}, u32[]{:S(2)}) collective-permute-start(f32[5,1,64,1,128]{4,1,0,3,2:T(1,128)} %get-tuple-element.12), channel_id=1, source_target_pairs={{0,64},{64,128},{128,192},{1,65},{65,129},{129,193},{2,66},{66,130... | collective-permute-start | bytes 491528 | tf_op jit(solution)/shard_map/ppermute | solution.py:21
  (20 other events, 33.3 us)
where the time goes:
time: 174 us; the launch traced here: 173 us
  starting transfers between devices  93.9 us (54%)
  other arithmetic  36.9 us (21%)
  local copies, waits for them, and re-layouts  34.4 us (20%)
  waiting for transfers between devices  6 us (3%)
    ppermute x12, starting transfers between devices, from_behind(): return lax.ppermute(block, axis, route)  56.6 us
    concatenate x12, other arithmetic, body(): jnp.concatenate([adjoint, potential], 0)  15 us
    ppermute x3, starting transfers between devices, extended(): lax.ppermute(lax.slice_in_dim(block, block.shape[dim] - width, None, axis...  14.3 us
    all_to_all x1, starting transfers between devices, body(): lax.all_to_all(pencil, 'yz', split_axis=2, concat_axis=1, tiled=True)[None]  12.5 us
    ppermute x3, starting transfers between devices, extended(): lax.ppermute(lax.slice_in_dim(block, 0, width, axis=dim), axis, backward)  10.5 us
    unnamed x51, local copies, waits for them, and re-layouts  7.7 us
    add x3, other arithmetic, advance(): return adjoint + change  7.53 us
    broadcast_in_dim x3, local copies, waits for them, and re-layouts, faces(): z_minus = jnp.concatenate([below[..., None], field[..., :-1]], 4)  6.1 us
  transfers between devices with their start and end apart: 19, of which 1 were waited for; matrix products, arithmetic and copies ran while one was open for 13% of the time, Pallas kernels for 0%

commit v1 on v0

v1 whole, which is shorter than its diff:
```python
import functools
import math

import jax
import jax.numpy as jnp
import ml_dtypes
import numpy as np
from jax import lax
from jax.experimental import pallas as pl
from jax.experimental.pallas import tpu as pltpu
from jax.sharding import PartitionSpec as P

SPECIES = 4
STEPS = 3
SCREEN = 1.0
MESH = pl.DeviceIdType.MESH

PZ, PY = 4, 16
NYZ = PZ * PY
BX, BY, BZ = 8, 64, 128
MODES = 512
TOP, ROWS = 8, 80
OWN = slice(TOP, TOP + BY)
F32, BF16 = jnp.float32, jnp.bfloat16


def base_table():
    half = MODES // 2
    modes = np.arange(half)[:, None]
    cells = np.arange(BZ)[None, :]
    angle = (modes * cells % MODES) * (2.0 * math.pi / MODES)
    theta = modes * (2.0 * math.pi / MODES)
    green = 1.0 / (1.0 + SCREEN * theta * theta)
    table = np.concatenate([np.cos(angle) * green, np.sin(angle) * green], 0)
    high = table.astype(np.float32).astype(ml_dtypes.bfloat16)
    low = (table - high.astype(np.float64)).astype(ml_dtypes.bfloat16)
    return high, low


def quarter_turned(a, b, turns):
    if turns == 0:
        return a, b
    k = lax.broadcasted_iota(jnp.int32, a.shape, 1)
    odd = (k & 1) == 1
    if turns == 2:
        return jnp.where(odd, -a, a), jnp.where(odd, -b, b)
    third = (k & 2) == 2
    if turns == 3:
        third = third != odd
    cos_part = jnp.where(odd, b, a)
    sin_part = jnp.where(odd, a, b)
    cos_part = jnp.where(third, -cos_part, cos_part)
    sin_part = jnp.where(third != odd, -sin_part, sin_part)
    return cos_part, sin_part


def lanes():
    return lax.broadcasted_iota(jnp.int32, (8, BZ), 1)


def pack_plane(plane, x):
    lane = lanes()
    parts = [plane[8 * r : 8 * r + 8] for r in range(8)]
    width = 2
    while len(parts) > 1:
        moved = (lane >= width - 1) & (lane < 2 * width - 1)
        parts = [
            jnp.where(moved, pltpu.roll(right, width, 1), left)
            for left, right in zip(parts[::2], parts[1::2])
        ]
        width *= 2
    whole = parts[0]
    if x > 0:
        whole = pltpu.roll(whole, 16 * x, 1)
    return whole


def merged(packed, whole, x):
    lane = lanes()
    if x == 0:
        return whole
    return jnp.where((lane >= 16 * x - 1) & (lane < 16 * x + 15), whole, packed)


def unpack_plane(packed, x):
    if x > 0:
        packed = pltpu.roll(packed, BZ - 16 * x, 1)
    return jnp.concatenate(
        [packed] + [pltpu.roll(packed, BZ - 2 * r, 1) for r in range(1, 8)], 0
    )


def slab_kernel(
    lam_hbm, dif_hbm, vel_hbm, cm_hbm, high_hbm, low_hbm, out_hbm,
    l0, l1, l2, l3, dif, vel, drift, slope, pot, cm, high, low,
    product, sendbuf, recv, y_out, y_in, z_out, z_in,
    load_sem, a2a_send, a2a_recv, halo_send, halo_recv,
):
    gx = lax.axis_index("gx")
    me = lax.axis_index("yz")
    ngx = lax.axis_size("gx")
    p = lax.rem(me, PY)
    zb = lax.div(me, PY)
    has = {
        "x+": gx < ngx - 1, "x-": gx > 0,
        "y+": p < PY - 1, "y-": p > 0,
        "z+": zb < PZ - 1, "z-": zb > 0,
    }
    ids = {
        "x+": {"gx": gx + 1}, "x-": {"gx": gx - 1},
        "y+": {"yz": me + 1}, "y-": {"yz": me - 1},
        "z+": {"yz": me + PY}, "z-": {"yz": me - PY},
    }
    ways = ("x+", "x-", "y+", "y-", "z+", "z-")
    back = {"x+": "x-", "x-": "x+", "y+": "y-", "y-": "y+", "z+": "z-", "z-": "z+"}

    own = (slice(None), slice(1, 1 + BX), OWN)
    loads = [
        pltpu.make_async_copy(cm_hbm, cm, load_sem.at[0]),
        pltpu.make_async_copy(high_hbm, high, load_sem.at[1]),
        pltpu.make_async_copy(low_hbm, low, load_sem.at[2]),
        pltpu.make_async_copy(lam_hbm, l0.at[:, pl.ds(1, BX), pl.ds(TOP, BY), :], load_sem.at[3]),
        pltpu.make_async_copy(dif_hbm, dif, load_sem.at[4]),
        pltpu.make_async_copy(vel_hbm, vel, load_sem.at[5]),
    ]
    for load in loads:
        load.start()

    barrier = pltpu.get_barrier_semaphore()

    @pl.loop(1, NYZ)
    def _(k):
        pl.semaphore_signal(
            barrier, inc=1, device_id={"yz": lax.rem(me + k, NYZ)}, device_id_type=MESH
        )

    for way in ("x+", "x-"):
        @pl.when(has[way])
        def _():
            pl.semaphore_signal(barrier, inc=1, device_id=ids[way], device_id_type=MESH)

    zero = jnp.zeros((BY, BZ), F32)

    @pl.when(jnp.logical_not(has["x-"]))
    def _():
        for ref in (l0, l1, l2):
            for s in range(SPECIES):
                ref[s, 0, OWN, :] = zero
        pot[0, 0, OWN, :] = zero

    @pl.when(jnp.logical_not(has["x+"]))
    def _():
        for ref in (l0, l1, l2):
            for s in range(SPECIES):
                ref[s, BX + 1, OWN, :] = zero
        pot[0, BX + 1, OWN, :] = zero

    for load in loads[:3]:
        load.wait()
    charge = cm[...].reshape(BX * PY, MODES)
    a, b = charge[:, : MODES // 2], charge[:, MODES // 2 :]
    dot = functools.partial(jnp.dot, preferred_element_type=F32)
    for turns in range(PZ):
        total = None
        for half, part in enumerate(quarter_turned(a, b, turns)):
            rows = slice(half * MODES // 2, (half + 1) * MODES // 2)
            part_high = part.astype(BF16)
            part_low = (part - part_high.astype(F32)).astype(BF16)
            term = dot(part_high, high[rows, :]) + (
                dot(part_low, high[rows, :]) + dot(part_high, low[rows, :])
            )
            total = term if total is None else total + term
        product[...] = total
        for q in range(PY):
            sendbuf[pl.ds((turns * PY + q) * BX, BX), :] = product[pl.ds(q, BX, stride=PY), :]

    pl.semaphore_wait(
        barrier,
        NYZ - 1 + has["x+"].astype(jnp.int32) + has["x-"].astype(jnp.int32),
    )

    def tile(ref, index):
        return ref.at[pl.ds(pl.multiple_of(index * BX, BX), BX), :]

    @pl.loop(1, NYZ)
    def _(k):
        peer = lax.rem(me + k, NYZ)
        pltpu.make_async_remote_copy(
            src_ref=tile(sendbuf, peer),
            dst_ref=tile(recv, me),
            send_sem=a2a_send,
            recv_sem=a2a_recv,
            device_id={"yz": peer},
            device_id_type=MESH,
        ).start()

    mine = pl.ds(pl.multiple_of(me * BX, BX), BX)
    recv[mine, :] = sendbuf[mine, :]

    def halo_copy(stage, way, fields, y_src=None):
        n = fields.shape[0]
        number = ways.index(way)
        if way == "x+":
            src = fields.at[:, BX, pl.ds(TOP, BY), :]
            dst = fields.at[:, 0, pl.ds(TOP, BY), :]
        elif way == "x-":
            src = fields.at[:, 1, pl.ds(TOP, BY), :]
            dst = fields.at[:, BX + 1, pl.ds(TOP, BY), :]
        elif way[0] == "y":
            src = y_out.at[stage, number - 2, pl.ds(0, n)]
            dst = y_in.at[stage, number - 2, pl.ds(0, n)]
        else:
            src = z_out.at[stage, pl.ds(0, n)]
            dst = z_in.at[stage, number - 4, pl.ds(0, n)]
        return pltpu.make_async_remote_copy(
            src_ref=src, dst_ref=dst,
            send_sem=halo_send.at[stage, number],
            recv_sem=halo_recv.at[stage, number],
            device_id=ids[way], device_id_type=MESH,
        )

    def start(stage, fields, which=ways):
        for way in which:
            @pl.when(has[way])
            def _():
                halo_copy(stage, way, fields).start()

    def receive(stage, fields, which=ways):
        for way in which:
            @pl.when(has[back[way]])
            def _():
                halo_copy(stage, way, fields).wait_recv()

    def finish(stage, fields):
        for way in ways:
            @pl.when(has[way])
            def _():
                halo_copy(stage, way, fields).wait_send()

    def stage_rims(stage, s, planes, fields):
        packed = None
        for x in range(BX):
            plane = planes(x)
            y_out[stage, 0, s, x : x + 1, :] = plane[BY - 1 :]
            y_out[stage, 1, s, x : x + 1, :] = plane[:1]
            packed = merged(packed, pack_plane(plane, x), x)
        z_out[stage, s] = packed

    def place_rims(stage, s, fields):
        low_rows = jnp.where(has["y-"], y_in[stage, 0, s], 0.0)
        high_rows = jnp.where(has["y+"], y_in[stage, 1, s], 0.0)
        for x in range(BX):
            fields[s, x + 1, TOP - 1 : TOP, :] = low_rows[x : x + 1]
            fields[s, x + 1, TOP + BY : TOP + BY + 1, :] = high_rows[x : x + 1]
        below = jnp.where(has["z-"], z_in[stage, 0, s], 0.0)
        above = jnp.where(has["z+"], z_in[stage, 1, s], 0.0)
        even = (lanes() & 1) == 0
        return jnp.where(even, pltpu.roll(below, 1, 1), pltpu.roll(above, BZ - 1, 1))

    lane = lax.broadcasted_iota(jnp.int32, (BY, BZ), 1)

    def near(fields, s, x, packed):
        centre = fields[s, x + 1, OWN, :]
        edge = unpack_plane(packed, x)
        z_plus = jnp.where(lane == BZ - 1, edge, pltpu.roll(centre, BZ - 1, 1))
        z_minus = jnp.where(lane == 0, edge, pltpu.roll(centre, 1, 1))
        return (
            centre,
            fields[s, x + 2, OWN, :], fields[s, x, OWN, :],
            fields[s, x + 1, TOP + 1 : TOP + BY + 1, :], fields[s, x + 1, TOP - 1 : TOP + BY - 1, :],
            z_plus, z_minus,
        )

    for load in loads[3:]:
        load.wait()

    @pl.loop(0, SPECIES)
    def _(s):
        stage_rims(0, s, lambda x: l0[s, x + 1, OWN, :], l0)

    start(0, l0)

    pltpu.make_async_copy(
        recv.at[pl.ds(0, (NYZ - 1) * BX), :], recv.at[pl.ds(0, (NYZ - 1) * BX), :], a2a_recv
    ).wait()
    y_out[1, 0, 0] = recv[pl.ds((BY - 1) * BX, BX), :]
    y_out[1, 1, 0] = recv[pl.ds(0, BX), :]
    start(1, pot, ("y+", "y-"))
    packed = None
    for x in (0, BX - 1):
        pot[0, x + 1, OWN, :] = recv[pl.ds(x, BY, stride=BX), :]
    start(1, pot, ("x+", "x-"))
    for x in range(1, BX - 1):
        pot[0, x + 1, OWN, :] = recv[pl.ds(x, BY, stride=BX), :]
    for x in range(BX):
        packed = merged(packed, pack_plane(pot[0, x + 1, OWN, :], x), x)
    z_out[1, 0] = packed
    start(1, pot, ("z+", "z-"))
    receive(1, pot)
    packed = place_rims(1, 0, pot)
    for x in range(BX):
        _, x_plus, x_minus, y_plus, y_minus, z_plus, z_minus = near(pot, 0, x, packed)
        slope[0, x] = x_plus - x_minus
        slope[1, x] = y_plus - y_minus
        slope[2, x] = z_plus - z_minus

    fields = (l0, l1, l2, l3)
    stages = (0, 2, 3)
    for step in range(STEPS):
        now, later, stage = fields[step], fields[step + 1], stages[step]
        receive(stage, now)

        @pl.loop(0, SPECIES)
        def _(s):
            valence = jnp.where(s == 0, 1.0, jnp.where(s == 2, 2.0, -1.0)).astype(F32)
            packed = place_rims(stage, s, now)
            out = None
            for x in range(BX):
                centre, x_plus, x_minus, y_plus, y_minus, z_plus, z_minus = near(now, s, x, packed)
                diffusion = dif[s, x]
                if step == 0:
                    scaled = (0.25 * valence) * diffusion
                    along = [0.5 * vel[axis, x] - scaled * slope[axis, x] for axis in range(3)]
                    for axis in range(3):
                        drift[axis, s, x] = along[axis]
                else:
                    along = [drift[axis, s, x] for axis in range(3)]
                spread = x_plus + x_minus + (y_plus + y_minus) + (z_plus + z_minus) - 6.0 * centre
                change = diffusion * spread
                change = change + along[0] * (x_plus - x_minus)
                change = change + along[1] * (y_plus - y_minus)
                change = change + along[2] * (z_plus - z_minus)
                new = centre + change
                if step == STEPS - 1:
                    later[s, x] = new
                else:
                    later[s, x + 1, OWN, :] = new
                    y_out[stages[step + 1], 0, s, x : x + 1, :] = new[BY - 1 :]
                    y_out[stages[step + 1], 1, s, x : x + 1, :] = new[:1]
                    out = merged(out, pack_plane(new, x), x)
            if step < STEPS - 1:
                z_out[stages[step + 1], s] = out

        if step < STEPS - 1:
            start(stages[step + 1], later)

    store = pltpu.make_async_copy(l3, out_hbm, load_sem.at[0])
    store.start()

    pltpu.make_async_copy(
        sendbuf.at[pl.ds(0, (NYZ - 1) * BX), :], sendbuf.at[pl.ds(0, (NYZ - 1) * BX), :], a2a_send
    ).wait()
    for stage, ref in ((0, l0), (1, pot), (2, l1), (3, l2)):
        finish(stage, ref)
    store.wait()


def body(terminal_adjoint, diffusivity, velocity, charge_modes):
    high, low = base_table()
    brick = (SPECIES, BX, BY, BZ)
    padded = (SPECIES, BX + 2, ROWS, BZ)
    anywhere = pl.BlockSpec(memory_space=pl.ANY)
    out = pl.pallas_call(
        slab_kernel,
        out_shape=jax.ShapeDtypeStruct(brick, F32),
        in_specs=[anywhere] * 6,
        out_specs=anywhere,
        scratch_shapes=[
            pltpu.VMEM(padded, F32), pltpu.VMEM(padded, F32), pltpu.VMEM(padded, F32),
            pltpu.VMEM(brick, F32),
            pltpu.VMEM(brick, F32),
            pltpu.VMEM((3, BX, BY, BZ), F32),
            pltpu.VMEM((3,) + brick, F32),
            pltpu.VMEM((3, BX, BY, BZ), F32),
            pltpu.VMEM((1, BX + 2, ROWS, BZ), F32),
            pltpu.VMEM((BX, PY, MODES), F32),
            pltpu.VMEM((MODES, BZ), BF16), pltpu.VMEM((MODES, BZ), BF16),
            pltpu.VMEM((BX * PY, BZ), F32),
            pltpu.VMEM((NYZ * BX, BZ), F32),
            pltpu.VMEM((NYZ * BX, BZ), F32),
            pltpu.VMEM((4, 2, SPECIES, BX, BZ), F32),
            pltpu.VMEM((4, 2, SPECIES, BX, BZ), F32),
            pltpu.VMEM((4, SPECIES, 8, BZ), F32),
            pltpu.VMEM((4, 2, SPECIES, 8, BZ), F32),
            pltpu.SemaphoreType.DMA((6,)),
            pltpu.SemaphoreType.DMA,
            pltpu.SemaphoreType.DMA,
            pltpu.SemaphoreType.DMA((4, 6)),
            pltpu.SemaphoreType.DMA((4, 6)),
        ],
        compiler_params=pltpu.CompilerParams(
            collective_id=0, has_side_effects=True, vmem_limit_bytes=60 * 1024 * 1024
        ),
    )(
        terminal_adjoint.reshape(brick),
        diffusivity.reshape(brick),
        velocity.reshape((3,) + brick[1:]),
        charge_modes.reshape(BX, PY, MODES),
        jnp.asarray(high),
        jnp.asarray(low),
    )
    return out.reshape(terminal_adjoint.shape)


def solution(mesh):
    return jax.shard_map(
        body,
        mesh=mesh,
        in_specs=(
            P(None, "gx", None, "yz", None),
            P(None, "gx", None, "yz", None),
            P(None, "gx", None, "yz", None),
            P("gx", "yz", None, None),
        ),
        out_specs=P(None, "gx", None, "yz", None),
        check_vma=False,
    )
```

time: 174 us -> 47.3 us (0.27)
  the two profiles are of different devices: /device:TPU:9 before, /device:TPU:6 now
where the time goes in v1:
time: 47.3 us; the launch traced here: 47.2 us
  Pallas kernels  44.9 us (95%)
  local copies, waits for them, and re-layouts  2.31 us (5%)
    pallas_call x1, Pallas kernels, body(): pl.pallas_call(slab_kernel, out_shape=jax.ShapeDtypeStruct(brick, F32), i...  44.9 us
    unnamed x1, local copies, waits for them, and re-layouts  2.31 us

profile of v1, /device:TPU:6, one launch (start us, length us, event | category | flops | bytes accessed | tf_op | source)
XLA Modules:
  0.0 47.2 jit_solution(16094341830467521176)
XLA Ops:
  0.0 44.9 %shard_map.64 = f32[4,8,64,128]{3,2,1,0:T(8,128)} custom-call(f32[4,8,64,128]{3,2,1,0:T(8,128)} %bitcast.8, f32[4,8,64,128]{3,2,1,0:T(8,128)} %bitcast.9, f32[3,8,64,128]{3,2,1,0:T(8,128)} %bitcast.10, f32[8,16,512]{2,1,0:T(8,128)} %bitcast.11, bf16[512,128]{1,0:T(8,128)(2,1)} %constant.4.clone.high_hbm, bf16[512,128]{1,0:T(8,128)(2,1)} %constant.5.clone.low_hbm), custom_call_target="tpu_custom_call" | custom-call | tf_op jit(solution)/shard_map/pallas_call | solution.py:363
  44.9 2.3 %copy.9 = f32[4,8,64,1,128]{4,3,2,1,0:T(1,128)} copy(f32[4,8,64,1,128]{4,3,2,1,0:T(1,128)} %bitcast.7) | data formatting | bytes 2097152

commit v2 on v1

v2 whole, which is shorter than its diff:
```python
import functools
import math

import jax
import jax.numpy as jnp
import ml_dtypes
import numpy as np
from jax import lax
from jax.experimental import pallas as pl
from jax.experimental.pallas import tpu as pltpu
from jax.sharding import PartitionSpec as P

SPECIES = 4
STEPS = 3
SCREEN = 1.0
MESH = pl.DeviceIdType.MESH

PZ, PY = 4, 16
NYZ = PZ * PY
BX, BY, BZ = 8, 64, 128
MODES = 512
TOP, ROWS = 8, 80
TILE = BX + 1
ORDER = (0, BX - 1) + tuple(range(1, BX - 1))
PLACE = {x: row for row, x in enumerate(ORDER)}
FACE = 2
LOW, HIGH = NYZ, NYZ + 1
HALF = 32
F32, BF16 = jnp.float32, jnp.bfloat16


def base_table():
    half = MODES // 2
    modes = np.arange(half)[:, None]
    cells = np.arange(BZ)[None, :]
    angle = (modes * cells % MODES) * (2.0 * math.pi / MODES)
    theta = modes * (2.0 * math.pi / MODES)
    green = 1.0 / (1.0 + SCREEN * theta * theta)
    table = np.concatenate([np.cos(angle) * green, np.sin(angle) * green], 0)
    high = table.astype(np.float32).astype(ml_dtypes.bfloat16)
    low = (table - high.astype(np.float64)).astype(ml_dtypes.bfloat16)
    return high, low


def quarter_turned(a, b, turns):
    if turns == 0:
        return a, b
    k = lax.broadcasted_iota(jnp.int32, a.shape, 1)
    odd = (k & 1) == 1
    if turns == 2:
        return jnp.where(odd, -a, a), jnp.where(odd, -b, b)
    third = (k & 2) == 2
    if turns == 3:
        third = third != odd
    cos_part = jnp.where(odd, b, a)
    sin_part = jnp.where(odd, a, b)
    cos_part = jnp.where(third, -cos_part, cos_part)
    sin_part = jnp.where(third != odd, -sin_part, sin_part)
    return cos_part, sin_part


def lanes():
    return lax.broadcasted_iota(jnp.int32, (8, BZ), 1)


def pack_plane(plane, x):
    lane = lanes()
    parts = [plane[8 * r : 8 * r + 8] for r in range(8)]
    width = 2
    while len(parts) > 1:
        moved = (lane >= width - 1) & (lane < 2 * width - 1)
        parts = [
            jnp.where(moved, pltpu.roll(right, width, 1), left)
            for left, right in zip(parts[::2], parts[1::2])
        ]
        width *= 2
    whole = parts[0]
    if x > 0:
        whole = pltpu.roll(whole, 16 * x, 1)
    return whole


def merged(packed, whole, x):
    lane = lanes()
    if x == 0:
        return whole
    return jnp.where((lane >= 16 * x - 1) & (lane < 16 * x + 15), whole, packed)


def unpack_plane(packed, x):
    lane = lanes()
    rim = (lane == 0) | (lane == BZ - 1)
    shifts = [(BZ - 16 * x - 2 * r) % BZ for r in range(8)]
    moved = [pltpu.roll(packed, shift, 1) if shift else packed for shift in shifts]
    return jnp.concatenate([jnp.where(rim, part, 0.0) for part in moved], 0)


def padded_row(x):
    return (x + 1) * ROWS + TOP


def slab_kernel(
    lam_hbm, dif_hbm, vel_hbm, cm_hbm, high_hbm, low_hbm, l3,
    l0, l1, l2, dif, vel, along, base, grad, slope, pot, cm, high, low,
    product, sendbuf, recv, x_in, y_out, y_in, z_out, z_in,
    load_sem, lam_sem, store_sem, a2a_send, a2a_recv, edge_send, edge_recv, halo_send, halo_recv,
):
    gx = lax.axis_index("gx")
    me = lax.axis_index("yz")
    ngx = lax.axis_size("gx")
    p = lax.rem(me, PY)
    zb = lax.div(me, PY)
    mx, mz, my = lax.rem(me, 4), lax.rem(lax.div(me, 4), 8), lax.div(me, 32)
    has = {
        "x+": gx < ngx - 1, "x-": gx > 0,
        "y+": p < PY - 1, "y-": p > 0,
        "z+": zb < PZ - 1, "z-": zb > 0,
    }
    ids = {
        "x+": {"gx": gx + 1}, "x-": {"gx": gx - 1},
        "y+": {"yz": me + 1}, "y-": {"yz": me - 1},
        "z+": {"yz": me + PY}, "z-": {"yz": me - PY},
    }
    ways = ("z+", "z-", "x+", "x-", "y+", "y-")
    back = {"x+": "x-", "x-": "x+", "y+": "y-", "y-": "y+", "z+": "z-", "z-": "z+"}

    def partners(act):
        @pl.loop(0, 8)
        def _(j):
            step = lax.div(j + 1, 2)
            dz = 4 + jnp.where(lax.rem(j, 2) == 0, -step, step)
            z = lax.rem(mz + dz + 8, 8)
            for dx in (2, 1, 3, 0):
                for dy in (1, 0):
                    x = lax.rem(mx + dx, 4) if dx else mx
                    y = 1 - my if dy else my
                    peer = (y * 8 + z) * 4 + x
                    if dx or dy:
                        act(peer)
                    else:
                        pl.when(j < 7)(functools.partial(act, peer))

    barrier = pltpu.get_barrier_semaphore()
    partners(
        lambda peer: pl.semaphore_signal(
            barrier, inc=1, device_id={"yz": peer}, device_id_type=MESH
        )
    )
    for way in ("x+", "x-"):
        @pl.when(has[way])
        def _():
            pl.semaphore_signal(barrier, inc=1, device_id=ids[way], device_id_type=MESH)

    loads = [
        pltpu.make_async_copy(cm_hbm, cm, load_sem.at[0]),
        pltpu.make_async_copy(high_hbm, high, load_sem.at[1]),
        pltpu.make_async_copy(low_hbm, low, load_sem.at[2]),
        pltpu.make_async_copy(dif_hbm, dif, load_sem.at[3]),
        pltpu.make_async_copy(vel_hbm, vel, load_sem.at[4]),
    ]
    lam_loads = [
        pltpu.make_async_copy(lam_hbm.at[:, x], l0.at[:, pl.ds(padded_row(x), BY), :], lam_sem.at[x])
        for x in range(BX)
    ]
    for load in loads[:3] + lam_loads + loads[3:]:
        load.start()

    zero = jnp.zeros((BY, BZ), F32)
    line = jnp.zeros((BX, BZ), F32)
    for ref in (l0, l1, l2):
        @pl.loop(0, SPECIES)
        def _(s):
            ref[s, TOP : TOP + BY, :] = zero
            ref[s, padded_row(BX) : padded_row(BX) + BY, :] = zero
            ref[s, pl.ds(padded_row(0) - 1, BX, stride=ROWS), :] = line
            ref[s, pl.ds(padded_row(0) + BY, BX, stride=ROWS), :] = line

    for side, way in enumerate(("-", "+")):
        @pl.when(jnp.logical_not(has["x" + way]))
        def _():
            for stage in range(STEPS):
                for s in range(SPECIES):
                    x_in[stage, side, s] = zero
            face = TOP if side == 0 else padded_row(BX)
            pot[0, face : face + BY, :] = zero

        @pl.when(jnp.logical_not(has["y" + way]))
        def _():
            for stage in range(STEPS):
                for s in range(SPECIES):
                    y_in[stage, side, s] = line
            recv[(LOW + side) * TILE : (LOW + side) * TILE + BX, :] = line

        @pl.when(jnp.logical_not(has["z" + way]))
        def _():
            for stage in range(STEPS):
                for s in range(SPECIES):
                    z_in[stage, side, s] = line

    for load in loads[:3]:
        load.wait()
    charge = cm[...].reshape(BX * PY, MODES)
    a, b = charge[:, : MODES // 2], charge[:, MODES // 2 :]
    dot = functools.partial(jnp.dot, preferred_element_type=F32)
    rims_of = []
    for turns in range(PZ):
        total = None
        for half, part in enumerate(quarter_turned(a, b, turns)):
            rows = slice(half * MODES // 2, (half + 1) * MODES // 2)
            part_high = part.astype(BF16)
            part_low = (part - part_high.astype(F32)).astype(BF16)
            term = dot(part_high, high[rows, :]) + (
                dot(part_low, high[rows, :]) + dot(part_high, low[rows, :])
            )
            total = term if total is None else total + term
        product[turns] = total
        turned = jnp.transpose(total)
        rims_of.append((turned[:1], turned[BZ - 1 :]))
        for q in range(PY):
            at = (turns * PY + q) * TILE
            tile = product[turns, pl.ds(q, BX, stride=PY), :]
            sendbuf[at : at + 1, :] = tile[:1]
            sendbuf[at + 1 : at + 2, :] = tile[BX - 1 :]
            sendbuf[at + 2 : at + BX, :] = tile[1 : BX - 1]
    nothing = jnp.zeros((1, BZ), F32)
    early = (lax.broadcasted_iota(jnp.int32, (1, BZ), 1) & (PY - 1)) < PY // 2
    for layer in range(PZ):
        below = rims_of[layer - 1][1] if layer > 0 else nothing
        above = rims_of[layer + 1][0] if layer < PZ - 1 else nothing
        above = pltpu.roll(above, PY // 2, 1)
        rows = (jnp.where(early, below, above), jnp.where(early, above, below))
        for q in range(PY):
            at = (layer * PY + q) * TILE + BX
            sendbuf[at : at + 1, :] = rows[q // (PY // 2)]

    pl.semaphore_wait(
        barrier,
        NYZ - 1 + has["x+"].astype(jnp.int32) + has["x-"].astype(jnp.int32),
    )

    def part(ref, index, start, count):
        return ref.at[pl.ds(index * TILE + start, count), :]

    def send_part(number, start, count):
        def act(peer):
            pltpu.make_async_remote_copy(
                src_ref=part(sendbuf, peer, start, count),
                dst_ref=part(recv, me, start, count),
                send_sem=a2a_send.at[number], recv_sem=a2a_recv.at[number],
                device_id={"yz": peer}, device_id_type=MESH,
            ).start()
        return act

    def bytes_of(ref, rows, sem):
        return pltpu.make_async_copy(ref.at[pl.ds(0, rows), :], ref.at[pl.ds(0, rows), :], sem)

    first, last = me == 0, me == NYZ - 1
    FACE_ROWS, REST_ROWS = (NYZ - 1) * FACE, (NYZ - 1) * (TILE - FACE)
    EDGE_ROWS = (PZ * (PY - 1) - 1) * BX

    def edge_copy(tile, peer, slot):
        return pltpu.make_async_remote_copy(
            src_ref=part(sendbuf, tile, 0, BX), dst_ref=part(recv, slot, 0, BX),
            send_sem=edge_send, recv_sem=edge_recv.at[slot - NYZ],
            device_id={"yz": peer}, device_id_type=MESH,
        )

    def send_rest(peer):
        send_part(1, FACE, TILE - FACE)(peer)
        q = lax.rem(peer, PY)
        pl.when(last & (q > 0))(lambda: edge_copy(peer - 1, peer, LOW).start())
        pl.when(first & (q < PY - 1))(lambda: edge_copy(peer + 1, peer, HIGH).start())

    partners(send_part(0, 0, FACE))

    def halo_copy(stage, way, fields):
        number = ways.index(way)
        side = 0 if way[1] == "+" else 1
        if way[0] == "x":
            src = fields.at[:, pl.ds(padded_row(BX - 1 if side == 0 else 0), BY), :]
            if stage == STEPS:
                dst = fields.at[:, pl.ds(TOP if side == 0 else padded_row(BX), BY), :]
            else:
                dst = x_in.at[stage, side]
        elif way[0] == "y":
            src, dst = y_out.at[stage, side], y_in.at[stage, side]
        else:
            src, dst = z_out.at[stage], z_in.at[stage, side]
        return pltpu.make_async_remote_copy(
            src_ref=src, dst_ref=dst,
            send_sem=halo_send.at[stage, number], recv_sem=halo_recv.at[stage, number],
            device_id=ids[way], device_id_type=MESH,
        )

    def start(stage, fields, which=ways):
        for way in which:
            pl.when(has[way])(lambda: halo_copy(stage, way, fields).start())

    def receive(stage, fields, which=ways):
        for way in which:
            pl.when(has[back[way]])(lambda: halo_copy(stage, way, fields).wait_recv())

    def finish(stage, fields, which=ways):
        for way in which:
            pl.when(has[way])(lambda: halo_copy(stage, way, fields).wait_send())

    def rims(stage, s, fields, planes=tuple(range(BX)), packed=None):
        for x in planes:
            plane = fields[s, padded_row(x) : padded_row(x) + BY, :]
            whole = pack_plane(plane, x)
            if packed is None:
                packed = whole
            else:
                packed = jnp.where((lanes() >= 16 * x - 1) & (lanes() < 16 * x + 15), whole, packed)
        return packed

    def finish_rims(stage, s, fields, packed):
        z_out[stage, s] = packed
        y_out[stage, 0, s] = fields[s, pl.ds(padded_row(0) + BY - 1, BX, stride=ROWS), :]
        y_out[stage, 1, s] = fields[s, pl.ds(padded_row(0), BX, stride=ROWS), :]

    def arrived_lanes(stage, s):
        even = (lanes() & 1) == 0
        below, above = z_in[stage, 0, s], z_in[stage, 1, s]
        return jnp.where(even, pltpu.roll(below, 1, 1), pltpu.roll(above, BZ - 1, 1))

    lane = lax.broadcasted_iota(jnp.int32, (BY, BZ), 1)
    at_low = lane == 0
    half_low, half_high = lane[:HALF] == 0, lane[:HALF] == BZ - 1

    def differences(fields, s, x, y):
        r = padded_row(x) + y
        centre = fields[s, r : r + HALF, :]
        x_plus, x_minus = fields[s, r + ROWS : r + ROWS + HALF, :], fields[s, r - ROWS : r - ROWS + HALF, :]
        y_plus, y_minus = fields[s, r + 1 : r + 1 + HALF, :], fields[s, r - 1 : r - 1 + HALF, :]
        z_plus = jnp.where(half_high, 0.0, pltpu.roll(centre, BZ - 1, 1))
        z_minus = jnp.where(half_low, 0.0, pltpu.roll(centre, 1, 1))
        spread = (x_plus + x_minus) + (y_plus + y_minus) + (z_plus + z_minus) - 6.0 * centre
        return centre, spread, (x_plus - x_minus, y_plus - y_minus, z_plus - z_minus)

    def quarter_valence(s):
        return jnp.where(s == 0, 0.25, jnp.where(s == 2, 0.5, -0.25)).astype(F32)

    for load in lam_loads:
        load.wait()

    @pl.loop(0, SPECIES)
    def _(s):
        finish_rims(0, s, l0, rims(0, s, l0))

    start(0, l0)
    partners(send_rest)
    mine = pl.ds(me * TILE, TILE)
    recv[mine, :] = sendbuf[mine, :]

    @pl.when(last)
    def _():
        recv[LOW * TILE : LOW * TILE + BX, :] = sendbuf[(NYZ - 2) * TILE : (NYZ - 2) * TILE + BX, :]

    @pl.when(first)
    def _():
        recv[HIGH * TILE : HIGH * TILE + BX, :] = sendbuf[TILE : TILE + BX, :]

    for load in loads[3:]:
        load.wait()

    @pl.loop(0, SPECIES)
    def _(s):
        charge_of = quarter_valence(s)
        for x in range(BX):
            for y in range(0, BY, HALF):
                rows = slice(x * BY + y, x * BY + y + HALF)
                centre, spread, diff = differences(l0, s, x, y)
                diffusion = dif[s, rows, :]
                scaled = charge_of * diffusion
                total = centre + diffusion * spread
                for axis in range(3):
                    total = total + (0.5 * vel[axis, rows, :]) * diff[axis]
                    grad[axis, s, rows, :] = scaled * diff[axis]
                base[s, rows, :] = total

    bytes_of(recv, FACE_ROWS, a2a_recv.at[0]).wait()

    def assemble(x):
        pot[0, padded_row(x) : padded_row(x) + BY, :] = recv[pl.ds(PLACE[x], BY, stride=TILE), :]

    assemble(0)
    assemble(BX - 1)
    start(STEPS, pot, ("x+", "x-"))

    def rim_terms(axis, side, s, rows):
        diffusion, flow = dif[s, rows, :], 0.5 * vel[axis, rows, :]
        scaled = quarter_valence(s) * diffusion
        if side == 0:
            return diffusion - flow, -scaled
        return diffusion + flow, scaled

    receive(0, l0)

    @pl.loop(0, SPECIES)
    def _(s):
        for side in (0, 1):
            x = (BX - 1) * side
            rows = slice(x * BY, (x + 1) * BY)
            value = x_in[0, side, s]
            to_base, to_grad = rim_terms(0, side, s, rows)
            base[s, rows, :] += to_base * value
            grad[0, s, rows, :] += to_grad * value
            rows = pl.ds((BY - 1) * side, BX, stride=BY)
            value = y_in[0, side, s]
            to_base, to_grad = rim_terms(1, side, s, rows)
            base[s, rows, :] += to_base * value
            grad[1, s, rows, :] += to_grad * value
        packed = arrived_lanes(0, s)
        for x in range(BX):
            rows = slice(x * BY, (x + 1) * BY)
            value = unpack_plane(packed, x)
            diffusion, flow = dif[s, rows, :], 0.5 * vel[2, rows, :]
            scaled = quarter_valence(s) * diffusion
            base[s, rows, :] += (diffusion + jnp.where(at_low, -flow, flow)) * value
            grad[2, s, rows, :] += jnp.where(at_low, -scaled, scaled) * value

    bytes_of(recv, REST_ROWS, a2a_recv.at[1]).wait()
    pl.when(has["y-"] & jnp.logical_not(last))(lambda: edge_copy(0, lax.rem(me + 1, NYZ), LOW).wait_recv())
    pl.when(has["y+"] & jnp.logical_not(first))(lambda: edge_copy(0, lax.rem(me + 1, NYZ), HIGH).wait_recv())
    for x in range(1, BX - 1):
        assemble(x)
    for x in range(BX):
        for side, row in ((0, padded_row(x) - 1), (1, padded_row(x) + BY)):
            at = (LOW + side) * TILE + PLACE[x]
            pot[0, row : row + 1, :] = recv[at : at + 1, :]
    z_rims = pltpu.roll(recv[pl.ds(BX, BY, stride=TILE), :], lax.rem(BZ - p, BZ), 1)

    def slopes(x):
        r = padded_row(x)
        rows = slice(x * BY, (x + 1) * BY)
        centre = pot[0, r : r + BY, :]
        low_rim = pltpu.roll(z_rims, (BZ - 16 * x) % BZ, 1) if x else z_rims
        high_rim = pltpu.roll(z_rims, (2 * BZ - 1 - 16 * x - 8) % BZ, 1)
        z_plus = jnp.where(lane == BZ - 1, high_rim, pltpu.roll(centre, BZ - 1, 1))
        z_minus = jnp.where(at_low, low_rim, pltpu.roll(centre, 1, 1))
        slope[0, rows, :] = pot[0, r + ROWS : r + ROWS + BY, :] - pot[0, r - ROWS : r - ROWS + BY, :]
        slope[1, rows, :] = pot[0, r + 1 : r + 1 + BY, :] - pot[0, r - 1 : r - 1 + BY, :]
        slope[2, rows, :] = z_plus - z_minus

    def first_step(s, x):
        rows = slice(x * BY, (x + 1) * BY)
        total = base[s, rows, :]
        for axis in range(3):
            total = total - slope[axis, rows, :] * grad[axis, s, rows, :]
        l1[s, padded_row(x) : padded_row(x) + BY, :] = total

    inner = tuple(range(1, BX - 1))
    for x in inner:
        slopes(x)

    @pl.loop(0, SPECIES)
    def _(s):
        for x in inner:
            first_step(s, x)
        z_out[1, s] = rims(1, s, l1, inner, line)

    receive(STEPS, pot, ("x+", "x-"))
    for x in (0, BX - 1):
        slopes(x)

    @pl.loop(0, SPECIES)
    def _(s):
        for x in (0, BX - 1):
            first_step(s, x)
        outer = rims(1, s, l1, (0, BX - 1))
        own = (lanes() >= 15) & (lanes() < 111)
        finish_rims(1, s, l1, jnp.where(own, z_out[1, s], outer))

    start(1, l1)

    def own_values(step, now, later, row_of):
        @pl.loop(0, SPECIES)
        def _(s):
            charge_of = quarter_valence(s)
            for x in range(BX):
                for y in range(0, BY, HALF):
                    rows = slice(x * BY + y, x * BY + y + HALF)
                    centre, spread, diff = differences(now, s, x, y)
                    diffusion = dif[s, rows, :]
                    total = centre + diffusion * spread
                    scaled = charge_of * diffusion
                    for axis in range(3):
                        if step == 1:
                            rate = 0.5 * vel[axis, rows, :] - scaled * slope[axis, rows, :]
                            along[axis, s, rows, :] = rate
                        else:
                            rate = along[axis, s, rows, :]
                        total = total + rate * diff[axis]
                    r = row_of(x) + y
                    later[s, r : r + HALF, :] = total

    def rim_values(step, later, row_of, after):
        @pl.loop(0, SPECIES)
        def _(s):
            apart = row_of(1) - row_of(0)
            for side in (0, 1):
                x = (BX - 1) * side
                rows = slice(x * BY, (x + 1) * BY)
                rate = along[0, s, rows, :]
                factor = dif[s, rows, :] + (rate if side else -rate)
                later[s, row_of(x) : row_of(x) + BY, :] += factor * x_in[step, side, s]
                rows = pl.ds((BY - 1) * side, BX, stride=BY)
                rate = along[1, s, rows, :]
                factor = dif[s, rows, :] + (rate if side else -rate)
                later[s, pl.ds(row_of(0) + (BY - 1) * side, BX, stride=apart), :] += factor * y_in[step, side, s]
            packed = arrived_lanes(step, s)
            for x in range(BX):
                rows = slice(x * BY, (x + 1) * BY)
                rate = along[2, s, rows, :]
                factor = dif[s, rows, :] + jnp.where(at_low, -rate, rate)
                later[s, row_of(x) : row_of(x) + BY, :] += factor * unpack_plane(packed, x)
            after(s)

    own_values(1, l1, l2, padded_row)
    receive(1, l1)
    rim_values(1, l2, padded_row, lambda s: finish_rims(2, s, l2, rims(2, s, l2)))
    start(2, l2)

    flat_row = lambda x: x * BY
    own_values(2, l2, l3, flat_row)
    receive(2, l2)
    rim_values(
        2, l3, flat_row,
        lambda s: None,
    )

    bytes_of(sendbuf, FACE_ROWS, a2a_send.at[0]).wait()
    bytes_of(sendbuf, REST_ROWS, a2a_send.at[1]).wait()
    pl.when(first | last)(lambda: bytes_of(sendbuf, EDGE_ROWS, edge_send).wait())
    for stage, ref in enumerate((l0, l1, l2)):
        finish(stage, ref)
    finish(STEPS, pot, ("x+", "x-"))


def hand_over_kernel(source, target, sems):
    copies = [
        pltpu.make_async_copy(source.at[s], target.at[s], sems.at[s]) for s in range(SPECIES)
    ]
    for copy in copies:
        copy.start()
    for copy in copies:
        copy.wait()


def body(terminal_adjoint, diffusivity, velocity, charge_modes):
    high, low = base_table()
    cells = BX * BY
    brick = (SPECIES, cells, BZ)
    padded = (SPECIES, (BX + 2) * ROWS, BZ)
    flow = (3, cells, BZ)
    anywhere = pl.BlockSpec(memory_space=pl.ANY)
    out = pl.pallas_call(
        slab_kernel,
        out_shape=pltpu.VMEM(brick, F32),
        in_specs=[anywhere] * 6,
        out_specs=pl.BlockSpec(memory_space=pltpu.VMEM),
        scratch_shapes=[
            pltpu.VMEM(padded, F32), pltpu.VMEM(padded, F32), pltpu.VMEM(padded, F32),
            pltpu.VMEM(brick, F32),
            pltpu.VMEM(flow, F32),
            pltpu.VMEM((3,) + brick, F32),
            pltpu.VMEM(brick, F32),
            pltpu.VMEM((3,) + brick, F32),
            pltpu.VMEM(flow, F32),
            pltpu.VMEM((1,) + padded[1:], F32),
            pltpu.VMEM((BX, PY, MODES), F32),
            pltpu.VMEM((MODES, BZ), BF16), pltpu.VMEM((MODES, BZ), BF16),
            pltpu.VMEM((PZ, BX * PY, BZ), F32),
            pltpu.VMEM((NYZ * TILE, BZ), F32),
            pltpu.VMEM(((NYZ + 2) * TILE, BZ), F32),
            pltpu.VMEM((STEPS, 2, SPECIES, BY, BZ), F32),
            pltpu.VMEM((STEPS, 2, SPECIES, BX, BZ), F32),
            pltpu.VMEM((STEPS, 2, SPECIES, BX, BZ), F32),
            pltpu.VMEM((STEPS, SPECIES, 8, BZ), F32),
            pltpu.VMEM((STEPS, 2, SPECIES, 8, BZ), F32),
            pltpu.SemaphoreType.DMA((5,)),
            pltpu.SemaphoreType.DMA((BX,)),
            pltpu.SemaphoreType.DMA((SPECIES,)),
            pltpu.SemaphoreType.DMA((2,)),
            pltpu.SemaphoreType.DMA((2,)),
            pltpu.SemaphoreType.DMA,
            pltpu.SemaphoreType.DMA((2,)),
            pltpu.SemaphoreType.DMA((STEPS + 1, 6)),
            pltpu.SemaphoreType.DMA((STEPS + 1, 6)),
        ],
        compiler_params=pltpu.CompilerParams(
            collective_id=0, has_side_effects=True, vmem_limit_bytes=60 * 1024 * 1024
        ),
    )(
        terminal_adjoint.reshape(SPECIES, BX, BY, BZ),
        diffusivity.reshape(brick),
        velocity.reshape(flow),
        charge_modes.reshape(BX, PY, MODES),
        jnp.asarray(high),
        jnp.asarray(low),
    )
    return out.reshape(terminal_adjoint.shape)


def solution(mesh):
    return jax.shard_map(
        body,
        mesh=mesh,
        in_specs=(
            P(None, "gx", None, "yz", None),
            P(None, "gx", None, "yz", None),
            P(None, "gx", None, "yz", None),
            P("gx", "yz", None, None),
        ),
        out_specs=P(None, "gx", None, "yz", None),
        check_vma=False,
    )
```

time: 47.3 us -> 40.6 us (0.86)
  the two profiles are of different devices: /device:TPU:6 before, /device:TPU:1 now
where the time goes in v2:
time: 40.6 us; the launch traced here: 40.5 us
  Pallas kernels  39.5 us (97%)
  local copies, waits for them, and re-layouts  0.97 us (2%)
    pallas_call x1, Pallas kernels, body(): pl.pallas_call(slab_kernel, out_shape=pltpu.VMEM(brick, F32), in_specs=[a...  39.5 us
    unnamed x1, local copies, waits for them, and re-layouts  0.97 us

profile of v2, /device:TPU:1, one launch (start us, length us, event | category | flops | bytes accessed | tf_op | source)
XLA Modules:
  0.0 40.5 jit_solution(3145529782520243573)
XLA Ops:
  0.0 39.5 %shard_map.64 = f32[4,512,128]{2,1,0:T(8,128)S(1)} custom-call(f32[4,8,64,128]{3,2,1,0:T(8,128)} %bitcast.8, f32[4,512,128]{2,1,0:T(8,128)} %bitcast.9, f32[3,512,128]{2,1,0:T(8,128)} %bitcast.10, f32[8,16,512]{2,1,0:T(8,128)} %bitcast.11, bf16[512,128]{1,0:T(8,128)(2,1)} %constant.4.clone.high_hbm, bf16[512,128]{1,0:T(8,128)(2,1)} %constant.5.clone.low_hbm), custom_call_target="tpu_custom_call" | custom-call | tf_op jit(solution)/shard_map/pallas_call | solution.py:558
  39.5 1.0 %copy.9 = f32[4,8,64,1,128]{4,3,2,1,0:T(1,128)} copy(f32[4,8,64,1,128]{4,3,2,1,0:T(1,128)S(1)} %bitcast.7) | data formatting | bytes 2097152

commit v3 on v2

--- a/solution.py
+++ b/solution.py
@@ -21,8 +21,7 @@
 MODES = 512
 TOP, ROWS = 8, 80
 TILE = BX + 1
-ORDER = (0, BX - 1) + tuple(range(1, BX - 1))
-PLACE = {x: row for row, x in enumerate(ORDER)}
+PLACE = {x: (x + 1) % BX for x in range(BX)}
 FACE = 2
 LOW, HIGH = NYZ, NYZ + 1
 HALF = 32
@@ -102,15 +101,15 @@
 def slab_kernel(
     lam_hbm, dif_hbm, vel_hbm, cm_hbm, high_hbm, low_hbm, l3,
     l0, l1, l2, dif, vel, along, base, grad, slope, pot, cm, high, low,
-    product, sendbuf, recv, x_in, y_out, y_in, z_out, z_in,
-    load_sem, lam_sem, store_sem, a2a_send, a2a_recv, edge_send, edge_recv, halo_send, halo_recv,
+    product, sendbuf, recv, x_in, y_out, y_in, z_out, z_in, packs, factors, came,
+    load_sem, lam_sem, a2a_send, a2a_recv, edge_send, edge_recv, pass_send, pass_recv, halo_send, halo_recv,
 ):
     gx = lax.axis_index("gx")
     me = lax.axis_index("yz")
     ngx = lax.axis_size("gx")
-    p = lax.rem(me, PY)
-    zb = lax.div(me, PY)
-    mx, mz, my = lax.rem(me, 4), lax.rem(lax.div(me, 4), 8), lax.div(me, 32)
+    p = me & (PY - 1)
+    zb = me >> 4
+    mx, mz, my = me & 3, (me >> 2) & 7, me >> 5
     has = {
         "x+": gx < ngx - 1, "x-": gx > 0,
         "y+": p < PY - 1, "y-": p > 0,
@@ -127,12 +126,11 @@
     def partners(act):
         @pl.loop(0, 8)
         def _(j):
-            step = lax.div(j + 1, 2)
-            dz = 4 + jnp.where(lax.rem(j, 2) == 0, -step, step)
-            z = lax.rem(mz + dz + 8, 8)
+            step = (j + 1) >> 1
+            z = (mz + 4 + jnp.where((j & 1) == 0, -step, step)) & 7
             for dx in (2, 1, 3, 0):
                 for dy in (1, 0):
-                    x = lax.rem(mx + dx, 4) if dx else mx
+                    x = (mx + dx) & 3
                     y = 1 - my if dy else my
                     peer = (y * 8 + z) * 4 + x
                     if dx or dy:
@@ -194,8 +192,8 @@
         @pl.when(jnp.logical_not(has["z" + way]))
         def _():
             for stage in range(STEPS):
-                for s in range(SPECIES):
-                    z_in[stage, side, s] = line
+                for pair in range(SPECIES // 2):
+                    z_in[stage, side, pair] = line
 
     for load in loads[:3]:
         load.wait()
@@ -218,20 +216,17 @@
         rims_of.append((turned[:1], turned[BZ - 1 :]))
         for q in range(PY):
             at = (turns * PY + q) * TILE
-            tile = product[turns, pl.ds(q, BX, stride=PY), :]
-            sendbuf[at : at + 1, :] = tile[:1]
-            sendbuf[at + 1 : at + 2, :] = tile[BX - 1 :]
-            sendbuf[at + 2 : at + BX, :] = tile[1 : BX - 1]
+            sendbuf[pl.ds(at, BX), :] = pltpu.roll(product[turns, pl.ds(q, BX, stride=PY), :], 1, 0)
     nothing = jnp.zeros((1, BZ), F32)
-    early = (lax.broadcasted_iota(jnp.int32, (1, BZ), 1) & (PY - 1)) < PY // 2
+    odd = (lax.broadcasted_iota(jnp.int32, (1, BZ), 1) & 1) == 1
     for layer in range(PZ):
         below = rims_of[layer - 1][1] if layer > 0 else nothing
         above = rims_of[layer + 1][0] if layer < PZ - 1 else nothing
-        above = pltpu.roll(above, PY // 2, 1)
-        rows = (jnp.where(early, below, above), jnp.where(early, above, below))
+        above = pltpu.roll(above, BZ - 1, 1)
+        rows = (jnp.where(odd, above, below), jnp.where(odd, below, above))
         for q in range(PY):
             at = (layer * PY + q) * TILE + BX
-            sendbuf[at : at + 1, :] = rows[q // (PY // 2)]
+            sendbuf[at : at + 1, :] = rows[q % 2]
 
     pl.semaphore_wait(
         barrier,
@@ -255,23 +250,33 @@
         return pltpu.make_async_copy(ref.at[pl.ds(0, rows), :], ref.at[pl.ds(0, rows), :], sem)
 
     first, last = me == 0, me == NYZ - 1
-    FACE_ROWS, REST_ROWS = (NYZ - 1) * FACE, (NYZ - 1) * (TILE - FACE)
-    EDGE_ROWS = (PZ * (PY - 1) - 1) * BX
-
-    def edge_copy(tile, peer, slot):
+    special = first | last
+
+    def edge_tile(peer, side):
         return pltpu.make_async_remote_copy(
-            src_ref=part(sendbuf, tile, 0, BX), dst_ref=part(recv, slot, 0, BX),
-            send_sem=edge_send, recv_sem=edge_recv.at[slot - NYZ],
+            src_ref=part(sendbuf, peer, 0, TILE), dst_ref=part(recv, me, 0, TILE),
+            send_sem=edge_send, recv_sem=edge_recv.at[side],
             device_id={"yz": peer}, device_id_type=MESH,
         )
 
-    def send_rest(peer):
-        send_part(1, FACE, TILE - FACE)(peer)
-        q = lax.rem(peer, PY)
-        pl.when(last & (q > 0))(lambda: edge_copy(peer - 1, peer, LOW).start())
-        pl.when(first & (q < PY - 1))(lambda: edge_copy(peer + 1, peer, HIGH).start())
-
-    partners(send_part(0, 0, FACE))
+    def pass_on(side):
+        return pltpu.make_async_remote_copy(
+            src_ref=part(recv, (NYZ - 1) * (1 - side), 0, BX), dst_ref=part(recv, LOW + side, 0, BX),
+            send_sem=pass_send.at[side], recv_sem=pass_recv.at[side],
+            device_id=ids["y-" if side else "y+"], device_id_type=MESH,
+        )
+
+    mine = pl.ds(me * TILE, TILE)
+    recv[mine, :] = sendbuf[mine, :]
+    pl.when(last)(lambda: partners(lambda peer: edge_tile(peer, 0).start()))
+    pl.when(first)(lambda: partners(lambda peer: edge_tile(peer, 1).start()))
+    pl.when(jnp.logical_not(special))(lambda: partners(send_part(0, 0, FACE)))
+
+    def arrived(number, rows):
+        pl.when(special)(lambda: bytes_of(recv, (NYZ - 2) * rows, a2a_recv.at[number]).wait())
+        pl.when(jnp.logical_not(special))(
+            lambda: bytes_of(recv, (NYZ - 3) * rows, a2a_recv.at[number]).wait()
+        )
 
     def halo_copy(stage, way, fields):
         number = ways.index(way)
@@ -285,7 +290,7 @@
         elif way[0] == "y":
             src, dst = y_out.at[stage, side], y_in.at[stage, side]
         else:
-            src, dst = z_out.at[stage], z_in.at[stage, side]
+            src, dst = z_out.at[stage, side], z_in.at[stage, side]
         return pltpu.make_async_remote_copy(
             src_ref=src, dst_ref=dst,
             send_sem=halo_send.at[stage, number], recv_sem=halo_recv.at[stage, number],
@@ -304,25 +309,42 @@
         for way in which:
             pl.when(has[way])(lambda: halo_copy(stage, way, fields).wait_send())
 
-    def rims(stage, s, fields, planes=tuple(range(BX)), packed=None):
-        for x in planes:
-            plane = fields[s, padded_row(x) : padded_row(x) + BY, :]
-            whole = pack_plane(plane, x)
-            if packed is None:
-                packed = whole
-            else:
-                packed = jnp.where((lanes() >= 16 * x - 1) & (lanes() < 16 * x + 15), whole, packed)
+    def merge(packed, plane, x):
+        whole = pack_plane(plane, x)
+        if packed is None:
+            return whole
+        return jnp.where(((lanes() + 1 - 16 * x) & (BZ - 1)) < 16, whole, packed)
+
+    def packed_rims(plane_of):
+        packed = None
+        for x in range(BX):
+            packed = merge(packed, plane_of(x), x)
         return packed
 
-    def finish_rims(stage, s, fields, packed):
-        z_out[stage, s] = packed
-        y_out[stage, 0, s] = fields[s, pl.ds(padded_row(0) + BY - 1, BX, stride=ROWS), :]
-        y_out[stage, 1, s] = fields[s, pl.ds(padded_row(0), BX, stride=ROWS), :]
-
-    def arrived_lanes(stage, s):
-        even = (lanes() & 1) == 0
-        below, above = z_in[stage, 0, s], z_in[stage, 1, s]
-        return jnp.where(even, pltpu.roll(below, 1, 1), pltpu.roll(above, BZ - 1, 1))
+    even = (lanes() & 1) == 0
+
+    def send_lanes(stage, fields, packed):
+        for pair in range(SPECIES // 2):
+            one, two = packed(2 * pair), packed(2 * pair + 1)
+            z_out[stage, 0, pair] = jnp.where(even, pltpu.roll(two, 1, 1), one)
+            z_out[stage, 1, pair] = jnp.where(even, one, pltpu.roll(two, BZ - 1, 1))
+        start(stage, fields, ("z+", "z-"))
+
+    def receive_lanes(stage, fields):
+        receive(stage, fields, ("z+", "z-"))
+        for pair in range(SPECIES // 2):
+            below, above = z_in[stage, 0, pair], z_in[stage, 1, pair]
+            came[2 * pair] = jnp.where(even, pltpu.roll(below, 1, 1), pltpu.roll(above, BZ - 1, 1))
+            came[2 * pair + 1] = jnp.where(even, below, above)
+
+    def send_rows(stage, fields):
+        for s in range(SPECIES):
+            y_out[stage, 0, s] = fields[s, pl.ds(padded_row(0) + BY - 1, BX, stride=ROWS), :]
+            y_out[stage, 1, s] = fields[s, pl.ds(padded_row(0), BX, stride=ROWS), :]
+        start(stage, fields, ("y+", "y-"))
+
+    def own_plane(fields, s, x):
+        return fields[s, padded_row(x) : padded_row(x) + BY, :]
 
     lane = lax.broadcasted_iota(jnp.int32, (BY, BZ), 1)
     at_low = lane == 0
@@ -346,20 +368,12 @@
 
     @pl.loop(0, SPECIES)
     def _(s):
-        finish_rims(0, s, l0, rims(0, s, l0))
-
-    start(0, l0)
-    partners(send_rest)
-    mine = pl.ds(me * TILE, TILE)
-    recv[mine, :] = sendbuf[mine, :]
-
-    @pl.when(last)
-    def _():
-        recv[LOW * TILE : LOW * TILE + BX, :] = sendbuf[(NYZ - 2) * TILE : (NYZ - 2) * TILE + BX, :]
-
-    @pl.when(first)
-    def _():
-        recv[HIGH * TILE : HIGH * TILE + BX, :] = sendbuf[TILE : TILE + BX, :]
+        packs[s] = packed_rims(lambda x: own_plane(l0, s, x))
+
+    send_lanes(0, l0, lambda s: packs[s])
+    start(0, l0, ("x+", "x-"))
+    send_rows(0, l0)
+    pl.when(jnp.logical_not(special))(lambda: partners(send_part(1, FACE, TILE - FACE)))
 
     for load in loads[3:]:
         load.wait()
@@ -379,7 +393,11 @@
                     grad[axis, s, rows, :] = scaled * diff[axis]
                 base[s, rows, :] = total
 
-    bytes_of(recv, FACE_ROWS, a2a_recv.at[0]).wait()
+    pl.when(jnp.logical_not(last))(lambda: edge_tile(lax.rem(me + 1, NYZ), 0).wait_recv())
+    pl.when(jnp.logical_not(first))(lambda: edge_tile(lax.rem(me + 1, NYZ), 1).wait_recv())
+    pl.when(has["y+"])(lambda: pass_on(0).start())
+    pl.when(has["y-"])(lambda: pass_on(1).start())
+    arrived(0, FACE)
 
     def assemble(x):
         pot[0, padded_row(x) : padded_row(x) + BY, :] = recv[pl.ds(PLACE[x], BY, stride=TILE), :]
@@ -395,7 +413,8 @@
             return diffusion - flow, -scaled
         return diffusion + flow, scaled
 
-    receive(0, l0)
+    receive(0, l0, ("x+", "x-", "y+", "y-"))
+    receive_lanes(0, l0)
 
     @pl.loop(0, SPECIES)
     def _(s):
@@ -411,68 +430,58 @@
             to_base, to_grad = rim_terms(1, side, s, rows)
             base[s, rows, :] += to_base * value
             grad[1, s, rows, :] += to_grad * value
-        packed = arrived_lanes(0, s)
         for x in range(BX):
             rows = slice(x * BY, (x + 1) * BY)
-            value = unpack_plane(packed, x)
+            value = unpack_plane(came[s], x)
             diffusion, flow = dif[s, rows, :], 0.5 * vel[2, rows, :]
             scaled = quarter_valence(s) * diffusion
             base[s, rows, :] += (diffusion + jnp.where(at_low, -flow, flow)) * value
             grad[2, s, rows, :] += jnp.where(at_low, -scaled, scaled) * value
 
-    bytes_of(recv, REST_ROWS, a2a_recv.at[1]).wait()
-    pl.when(has["y-"] & jnp.logical_not(last))(lambda: edge_copy(0, lax.rem(me + 1, NYZ), LOW).wait_recv())
-    pl.when(has["y+"] & jnp.logical_not(first))(lambda: edge_copy(0, lax.rem(me + 1, NYZ), HIGH).wait_recv())
+    arrived(1, TILE - FACE)
     for x in range(1, BX - 1):
         assemble(x)
-    for x in range(BX):
-        for side, row in ((0, padded_row(x) - 1), (1, padded_row(x) + BY)):
-            at = (LOW + side) * TILE + PLACE[x]
-            pot[0, row : row + 1, :] = recv[at : at + 1, :]
-    z_rims = pltpu.roll(recv[pl.ds(BX, BY, stride=TILE), :], lax.rem(BZ - p, BZ), 1)
-
-    def slopes(x):
-        r = padded_row(x)
-        rows = slice(x * BY, (x + 1) * BY)
-        centre = pot[0, r : r + BY, :]
-        low_rim = pltpu.roll(z_rims, (BZ - 16 * x) % BZ, 1) if x else z_rims
-        high_rim = pltpu.roll(z_rims, (2 * BZ - 1 - 16 * x - 8) % BZ, 1)
-        z_plus = jnp.where(lane == BZ - 1, high_rim, pltpu.roll(centre, BZ - 1, 1))
-        z_minus = jnp.where(at_low, low_rim, pltpu.roll(centre, 1, 1))
-        slope[0, rows, :] = pot[0, r + ROWS : r + ROWS + BY, :] - pot[0, r - ROWS : r - ROWS + BY, :]
-        slope[1, rows, :] = pot[0, r + 1 : r + 1 + BY, :] - pot[0, r - 1 : r - 1 + BY, :]
-        slope[2, rows, :] = z_plus - z_minus
-
-    def first_step(s, x):
-        rows = slice(x * BY, (x + 1) * BY)
-        total = base[s, rows, :]
-        for axis in range(3):
-            total = total - slope[axis, rows, :] * grad[axis, s, rows, :]
-        l1[s, padded_row(x) : padded_row(x) + BY, :] = total
-
-    inner = tuple(range(1, BX - 1))
-    for x in inner:
-        slopes(x)
-
-    @pl.loop(0, SPECIES)
-    def _(s):
-        for x in inner:
-            first_step(s, x)
-        z_out[1, s] = rims(1, s, l1, inner, line)
-
+    pl.when(has["y-"])(lambda: pass_on(0).wait_recv())
+    pl.when(has["y+"])(lambda: pass_on(1).wait_recv())
+    for side, row in ((0, padded_row(0) - 1), (1, padded_row(0) + BY)):
+        at = (LOW + side) * TILE
+        pot[0, pl.ds(row, BX - 1, stride=ROWS), :] = recv[at + 1 : at + BX, :]
+        row += (BX - 1) * ROWS
+        pot[0, row : row + 1, :] = recv[at : at + 1, :]
+    z_rims = pltpu.roll(recv[pl.ds(BX, BY, stride=TILE), :], (BZ - p) & (BZ - 1), 1)
+
+    def first_step(x, packed):
+        rims_here = pltpu.roll(z_rims, BZ - 16 * x, 1) if x else z_rims
+        for y in range(0, BY, HALF):
+            r = padded_row(x) + y
+            rows = slice(x * BY + y, x * BY + y + HALF)
+            centre = pot[0, r : r + HALF, :]
+            rim = rims_here[y : y + HALF]
+            z_plus = jnp.where(half_high, rim, pltpu.roll(centre, BZ - 1, 1))
+            z_minus = jnp.where(half_low, rim, pltpu.roll(centre, 1, 1))
+            here = (
+                pot[0, r + ROWS : r + ROWS + HALF, :] - pot[0, r - ROWS : r - ROWS + HALF, :],
+                pot[0, r + 1 : r + 1 + HALF, :] - pot[0, r - 1 : r - 1 + HALF, :],
+                z_plus - z_minus,
+            )
+            for axis in range(3):
+                slope[axis, rows, :] = here[axis]
+            for s in range(SPECIES):
+                total = base[s, rows, :]
+                for axis in range(3):
+                    total = total - here[axis] * grad[axis, s, rows, :]
+                l1[s, r : r + HALF, :] = total
+        return [merge(packed[s], own_plane(l1, s, x), x) for s in range(SPECIES)]
+
+    packed = [line] * SPECIES
+    for x in range(1, BX - 1):
+        packed = first_step(x, packed)
     receive(STEPS, pot, ("x+", "x-"))
     for x in (0, BX - 1):
-        slopes(x)
-
-    @pl.loop(0, SPECIES)
-    def _(s):
-        for x in (0, BX - 1):
-            first_step(s, x)
-        outer = rims(1, s, l1, (0, BX - 1))
-        own = (lanes() >= 15) & (lanes() < 111)
-        finish_rims(1, s, l1, jnp.where(own, z_out[1, s], outer))
-
-    start(1, l1)
+        packed = first_step(x, packed)
+    send_lanes(1, l1, lambda s: packed[s])
+    start(1, l1, ("x+", "x-"))
+    send_rows(1, l1)
 
     def own_values(step, now, later, row_of):
         @pl.loop(0, SPECIES)
@@ -495,10 +504,11 @@
                     r = row_of(x) + y
                     later[s, r : r + HALF, :] = total
 
-    def rim_values(step, later, row_of, after):
+    def outer_values(step, later, row_of):
+        apart = row_of(1) - row_of(0)
+
         @pl.loop(0, SPECIES)
         def _(s):
-            apart = row_of(1) - row_of(0)
             for side in (0, 1):
                 x = (BX - 1) * side
                 rows = slice(x * BY, (x + 1) * BY)
@@ -509,30 +519,65 @@
                 rate = along[1, s, rows, :]
                 factor = dif[s, rows, :] + (rate if side else -rate)
                 later[s, pl.ds(row_of(0) + (BY - 1) * side, BX, stride=apart), :] += factor * y_in[step, side, s]
-            packed = arrived_lanes(step, s)
-            for x in range(BX):
-                rows = slice(x * BY, (x + 1) * BY)
-                rate = along[2, s, rows, :]
-                factor = dif[s, rows, :] + jnp.where(at_low, -rate, rate)
-                later[s, row_of(x) : row_of(x) + BY, :] += factor * unpack_plane(packed, x)
-            after(s)
+
+    def lane_factor(s, x):
+        rows = slice(x * BY, (x + 1) * BY)
+        rate = along[2, s, rows, :]
+        return dif[s, rows, :] + jnp.where(at_low, -rate, rate)
+
+    def lane_values(s, planes, later, row_of):
+        for x in planes:
+            later[s, row_of(x) : row_of(x) + BY, :] += lane_factor(s, x) * unpack_plane(came[s], x)
 
     own_values(1, l1, l2, padded_row)
-    receive(1, l1)
-    rim_values(1, l2, padded_row, lambda s: finish_rims(2, s, l2, rims(2, s, l2)))
-    start(2, l2)
+
+    @pl.loop(0, SPECIES)
+    def _(s):
+        factors[s] = packed_rims(lambda x: lane_factor(s, x))
+
+    receive(1, l1, ("y+", "y-", "x+", "x-"))
+    outer_values(1, l2, padded_row)
+
+    @pl.loop(0, SPECIES)
+    def _(s):
+        packs[s] = packed_rims(lambda x: own_plane(l2, s, x))
+
+    receive_lanes(1, l1)
+    send_lanes(2, l2, lambda s: packs[s] + factors[s] * came[s])
+
+    @pl.loop(0, SPECIES)
+    def _(s):
+        lane_values(s, (0, BX - 1), l2, padded_row)
+
+    start(2, l2, ("x+", "x-"))
+
+    @pl.loop(0, SPECIES)
+    def _(s):
+        lane_values(s, range(1, BX - 1), l2, padded_row)
+
+    send_rows(2, l2)
 
     flat_row = lambda x: x * BY
     own_values(2, l2, l3, flat_row)
-    receive(2, l2)
-    rim_values(
-        2, l3, flat_row,
-        lambda s: None,
-    )
-
-    bytes_of(sendbuf, FACE_ROWS, a2a_send.at[0]).wait()
-    bytes_of(sendbuf, REST_ROWS, a2a_send.at[1]).wait()
-    pl.when(first | last)(lambda: bytes_of(sendbuf, EDGE_ROWS, edge_send).wait())
+    receive(2, l2, ("y+", "y-", "x+", "x-"))
+    outer_values(2, l3, flat_row)
+    receive_lanes(2, l2)
+
+    @pl.loop(0, SPECIES)
+    def _(s):
+        lane_values(s, range(BX), l3, flat_row)
+
+    @pl.when(special)
+    def _():
+        bytes_of(sendbuf, (NYZ - 1) * TILE, edge_send).wait()
+
+    @pl.when(jnp.logical_not(special))
+    def _():
+        bytes_of(sendbuf, (NYZ - 1) * FACE, a2a_send.at[0]).wait()
+        bytes_of(sendbuf, (NYZ - 1) * (TILE - FACE), a2a_send.at[1]).wait()
+
+    pl.when(has["y+"])(lambda: pass_on(0).wait_send())
+    pl.when(has["y-"])(lambda: pass_on(1).wait_send())
     for stage, ref in enumerate((l0, l1, l2)):
         finish(stage, ref)
     finish(STEPS, pot, ("x+", "x-"))
@@ -577,14 +622,18 @@
             pltpu.VMEM((STEPS, 2, SPECIES, BY, BZ), F32),
             pltpu.VMEM((STEPS, 2, SPECIES, BX, BZ), F32),
             pltpu.VMEM((STEPS, 2, SPECIES, BX, BZ), F32),
-            pltpu.VMEM((STEPS, SPECIES, 8, BZ), F32),
-            pltpu.VMEM((STEPS, 2, SPECIES, 8, BZ), F32),
+            pltpu.VMEM((STEPS, 2, SPECIES // 2, 8, BZ), F32),
+            pltpu.VMEM((STEPS, 2, SPECIES // 2, 8, BZ), F32),
+            pltpu.VMEM((SPECIES, 8, BZ), F32),
+            pltpu.VMEM((SPECIES, 8, BZ), F32),
+            pltpu.VMEM((SPECIES, 8, BZ), F32),
             pltpu.SemaphoreType.DMA((5,)),
             pltpu.SemaphoreType.DMA((BX,)),
-            pltpu.SemaphoreType.DMA((SPECIES,)),
             pltpu.SemaphoreType.DMA((2,)),
             pltpu.SemaphoreType.DMA((2,)),
             pltpu.SemaphoreType.DMA,
+            pltpu.SemaphoreType.DMA((2,)),
+            pltpu.SemaphoreType.DMA((2,)),
             pltpu.SemaphoreType.DMA((2,)),
             pltpu.SemaphoreType.DMA((STEPS + 1, 6)),
             pltpu.SemaphoreType.DMA((STEPS + 1, 6)),

time: 40.6 us -> 36.8 us (0.906)
  Pallas kernels: 39.5 us -> 35.8 us
    pallas_call x1, Pallas kernels: 39.5 us -> 35.8 us  [body(): pl.pallas_call(slab_kernel, out_shape=pltpu.VMEM(brick, F32), in_specs=[a...]
where the time goes in v3:
time: 36.8 us
  Pallas kernels  35.8 us (97%)
  local copies, waits for them, and re-layouts  0.97 us (3%)
    pallas_call x1, Pallas kernels, body(): pl.pallas_call(slab_kernel, out_shape=pltpu.VMEM(brick, F32), in_specs=[a...  35.8 us
    unnamed x1, local copies, waits for them, and re-layouts  0.97 us

profile of v3, /device:TPU:1, one launch (start us, length us, event | category | flops | bytes accessed | tf_op | source)
XLA Modules:
  0.0 36.8 jit_solution(1188081240123547021)
XLA Ops:
  0.0 35.8 %shard_map.64 = f32[4,512,128]{2,1,0:T(8,128)S(1)} custom-call(f32[4,8,64,128]{3,2,1,0:T(8,128)} %bitcast.8, f32[4,512,128]{2,1,0:T(8,128)} %bitcast.9, f32[3,512,128]{2,1,0:T(8,128)} %bitcast.10, f32[8,16,512]{2,1,0:T(8,128)} %bitcast.11, bf16[512,128]{1,0:T(8,128)(2,1)} %constant.4.clone.high_hbm, bf16[512,128]{1,0:T(8,128)(2,1)} %constant.5.clone.low_hbm), custom_call_target="tpu_custom_call" | custom-call | tf_op jit(solution)/shard_map/pallas_call | solution.py:603
  35.8 1.0 %copy.9 = f32[4,8,64,1,128]{4,3,2,1,0:T(1,128)} copy(f32[4,8,64,1,128]{4,3,2,1,0:T(1,128)S(1)} %bitcast.7) | data formatting | bytes 2097152

commit v4 on v3

--- a/solution.py
+++ b/solution.py
@@ -62,36 +62,27 @@
     return lax.broadcasted_iota(jnp.int32, (8, BZ), 1)
 
 
-def pack_plane(plane, x):
+def pack(packed, tile_of, places):
+    slot = ((lanes() + 1) >> 1) & (BX * 8 - 1)
+    for x, r in places:
+        i = 8 * x + r
+        tile = tile_of(x, r)
+        packed = jnp.where(slot == i, pltpu.roll(tile, 2 * i, 1) if i else tile, packed)
+    return packed
+
+
+def unpack(packed, x, r):
     lane = lanes()
-    parts = [plane[8 * r : 8 * r + 8] for r in range(8)]
-    width = 2
-    while len(parts) > 1:
-        moved = (lane >= width - 1) & (lane < 2 * width - 1)
-        parts = [
-            jnp.where(moved, pltpu.roll(right, width, 1), left)
-            for left, right in zip(parts[::2], parts[1::2])
-        ]
-        width *= 2
-    whole = parts[0]
-    if x > 0:
-        whole = pltpu.roll(whole, 16 * x, 1)
-    return whole
-
-
-def merged(packed, whole, x):
-    lane = lanes()
-    if x == 0:
-        return whole
-    return jnp.where((lane >= 16 * x - 1) & (lane < 16 * x + 15), whole, packed)
-
-
-def unpack_plane(packed, x):
-    lane = lanes()
-    rim = (lane == 0) | (lane == BZ - 1)
-    shifts = [(BZ - 16 * x - 2 * r) % BZ for r in range(8)]
-    moved = [pltpu.roll(packed, shift, 1) if shift else packed for shift in shifts]
-    return jnp.concatenate([jnp.where(rim, part, 0.0) for part in moved], 0)
+    i = 8 * x + r
+    moved = pltpu.roll(packed, BZ - 2 * i, 1) if i else packed
+    return jnp.where((lane == 0) | (lane == BZ - 1), moved, 0.0)
+
+
+EVERY = tuple((x, r) for x in range(BX) for r in range(8))
+INNER = tuple((x, r) for x, r in EVERY if 0 < x < BX - 1 and 0 < r < 7)
+OUTER = tuple(place for place in EVERY if place not in INNER)
+FACES = tuple(place for place in EVERY if place[0] in (0, BX - 1))
+EDGES = tuple(place for place in OUTER if place not in FACES)
 
 
 def padded_row(x):
@@ -101,7 +92,7 @@
 def slab_kernel(
     lam_hbm, dif_hbm, vel_hbm, cm_hbm, high_hbm, low_hbm, l3,
     l0, l1, l2, dif, vel, along, base, grad, slope, pot, cm, high, low,
-    product, sendbuf, recv, x_in, y_out, y_in, z_out, z_in, packs, factors, came,
+    product, sendbuf, recv, x_in, y_out, y_in, z_out, z_in, pot_in, packs, factors, came,
     load_sem, lam_sem, a2a_send, a2a_recv, edge_send, edge_recv, pass_send, pass_recv, halo_send, halo_recv,
 ):
     gx = lax.axis_index("gx")
@@ -173,14 +164,18 @@
             ref[s, pl.ds(padded_row(0) - 1, BX, stride=ROWS), :] = line
             ref[s, pl.ds(padded_row(0) + BY, BX, stride=ROWS), :] = line
 
+    pot[0, TOP : TOP + BY, :] = zero
+    pot[0, padded_row(BX) : padded_row(BX) + BY, :] = zero
+    pot[0, pl.ds(padded_row(0) - 1, BX, stride=ROWS), :] = line
+    pot[0, pl.ds(padded_row(0) + BY, BX, stride=ROWS), :] = line
+
     for side, way in enumerate(("-", "+")):
         @pl.when(jnp.logical_not(has["x" + way]))
         def _():
             for stage in range(STEPS):
                 for s in range(SPECIES):
                     x_in[stage, side, s] = zero
-            face = TOP if side == 0 else padded_row(BX)
-            pot[0, face : face + BY, :] = zero
+            pot_in[side, 0] = zero
 
         @pl.when(jnp.logical_not(has["y" + way]))
         def _():
@@ -228,63 +223,13 @@
             at = (layer * PY + q) * TILE + BX
             sendbuf[at : at + 1, :] = rows[q % 2]
 
-    pl.semaphore_wait(
-        barrier,
-        NYZ - 1 + has["x+"].astype(jnp.int32) + has["x-"].astype(jnp.int32),
-    )
-
-    def part(ref, index, start, count):
-        return ref.at[pl.ds(index * TILE + start, count), :]
-
-    def send_part(number, start, count):
-        def act(peer):
-            pltpu.make_async_remote_copy(
-                src_ref=part(sendbuf, peer, start, count),
-                dst_ref=part(recv, me, start, count),
-                send_sem=a2a_send.at[number], recv_sem=a2a_recv.at[number],
-                device_id={"yz": peer}, device_id_type=MESH,
-            ).start()
-        return act
-
-    def bytes_of(ref, rows, sem):
-        return pltpu.make_async_copy(ref.at[pl.ds(0, rows), :], ref.at[pl.ds(0, rows), :], sem)
-
-    first, last = me == 0, me == NYZ - 1
-    special = first | last
-
-    def edge_tile(peer, side):
-        return pltpu.make_async_remote_copy(
-            src_ref=part(sendbuf, peer, 0, TILE), dst_ref=part(recv, me, 0, TILE),
-            send_sem=edge_send, recv_sem=edge_recv.at[side],
-            device_id={"yz": peer}, device_id_type=MESH,
-        )
-
-    def pass_on(side):
-        return pltpu.make_async_remote_copy(
-            src_ref=part(recv, (NYZ - 1) * (1 - side), 0, BX), dst_ref=part(recv, LOW + side, 0, BX),
-            send_sem=pass_send.at[side], recv_sem=pass_recv.at[side],
-            device_id=ids["y-" if side else "y+"], device_id_type=MESH,
-        )
-
-    mine = pl.ds(me * TILE, TILE)
-    recv[mine, :] = sendbuf[mine, :]
-    pl.when(last)(lambda: partners(lambda peer: edge_tile(peer, 0).start()))
-    pl.when(first)(lambda: partners(lambda peer: edge_tile(peer, 1).start()))
-    pl.when(jnp.logical_not(special))(lambda: partners(send_part(0, 0, FACE)))
-
-    def arrived(number, rows):
-        pl.when(special)(lambda: bytes_of(recv, (NYZ - 2) * rows, a2a_recv.at[number]).wait())
-        pl.when(jnp.logical_not(special))(
-            lambda: bytes_of(recv, (NYZ - 3) * rows, a2a_recv.at[number]).wait()
-        )
-
     def halo_copy(stage, way, fields):
         number = ways.index(way)
         side = 0 if way[1] == "+" else 1
         if way[0] == "x":
             src = fields.at[:, pl.ds(padded_row(BX - 1 if side == 0 else 0), BY), :]
             if stage == STEPS:
-                dst = fields.at[:, pl.ds(TOP if side == 0 else padded_row(BX), BY), :]
+                dst = pot_in.at[side]
             else:
                 dst = x_in.at[stage, side]
         elif way[0] == "y":
@@ -309,17 +254,11 @@
         for way in which:
             pl.when(has[way])(lambda: halo_copy(stage, way, fields).wait_send())
 
-    def merge(packed, plane, x):
-        whole = pack_plane(plane, x)
-        if packed is None:
-            return whole
-        return jnp.where(((lanes() + 1 - 16 * x) & (BZ - 1)) < 16, whole, packed)
-
-    def packed_rims(plane_of):
-        packed = None
-        for x in range(BX):
-            packed = merge(packed, plane_of(x), x)
-        return packed
+    def own_tiles(fields, s):
+        def tile_of(x, r):
+            row = padded_row(x) + 8 * r
+            return fields[s, row : row + 8, :]
+        return tile_of
 
     even = (lanes() & 1) == 0
 
@@ -343,11 +282,8 @@
             y_out[stage, 1, s] = fields[s, pl.ds(padded_row(0), BX, stride=ROWS), :]
         start(stage, fields, ("y+", "y-"))
 
-    def own_plane(fields, s, x):
-        return fields[s, padded_row(x) : padded_row(x) + BY, :]
-
     lane = lax.broadcasted_iota(jnp.int32, (BY, BZ), 1)
-    at_low = lane == 0
+    tile_low = lanes() == 0
     half_low, half_high = lane[:HALF] == 0, lane[:HALF] == BZ - 1
 
     def differences(fields, s, x, y):
@@ -363,48 +299,113 @@
     def quarter_valence(s):
         return jnp.where(s == 0, 0.25, jnp.where(s == 2, 0.5, -0.25)).astype(F32)
 
-    for load in lam_loads:
-        load.wait()
-
-    @pl.loop(0, SPECIES)
-    def _(s):
-        packs[s] = packed_rims(lambda x: own_plane(l0, s, x))
-
+    def pack_first():
+        for load in lam_loads:
+            load.wait()
+
+        @pl.loop(0, SPECIES // 2)
+        def _(pair):
+            for s in (2 * pair, 2 * pair + 1):
+                packs[s] = pack(line, own_tiles(l0, s), EVERY)
+
+    def first_own(begin, end):
+        @pl.loop(begin, end)
+        def _(s):
+            charge_of = quarter_valence(s)
+            for x in range(BX):
+                for y in range(0, BY, HALF):
+                    rows = slice(x * BY + y, x * BY + y + HALF)
+                    centre, spread, diff = differences(l0, s, x, y)
+                    diffusion = dif[s, rows, :]
+                    scaled = charge_of * diffusion
+                    total = centre + diffusion * spread
+                    for axis in range(3):
+                        total = total + (0.5 * vel[axis, rows, :]) * diff[axis]
+                        grad[axis, s, rows, :] = scaled * diff[axis]
+                    base[s, rows, :] = total
+
+    def load_rest():
+        for load in loads[3:]:
+            load.wait()
+
+    ahead = mz < 4
+    behind = jnp.logical_not(ahead)
+
+    @pl.when(ahead)
+    def _():
+        pack_first()
+        load_rest()
+        first_own(0, SPECIES)
+
+    pl.semaphore_wait(
+        barrier,
+        NYZ - 1 + has["x+"].astype(jnp.int32) + has["x-"].astype(jnp.int32),
+    )
+
+    def part(ref, index, start, count):
+        return ref.at[pl.ds(index * TILE + start, count), :]
+
+    def send_part(number, start, count):
+        def act(peer):
+            pltpu.make_async_remote_copy(
+                src_ref=part(sendbuf, peer, start, count),
+                dst_ref=part(recv, me, start, count),
+                send_sem=a2a_send.at[number], recv_sem=a2a_recv.at[number],
+                device_id={"yz": peer}, device_id_type=MESH,
+            ).start()
+        return act
+
+    def bytes_of(ref, rows, sem):
+        return pltpu.make_async_copy(ref.at[pl.ds(0, rows), :], ref.at[pl.ds(0, rows), :], sem)
+
+    first, last = me == 0, me == NYZ - 1
+    special = first | last
+
+    def edge_tile(peer, side):
+        return pltpu.make_async_remote_copy(
+            src_ref=part(sendbuf, peer, FACE, TILE - FACE), dst_ref=part(recv, me, FACE, TILE - FACE),
+            send_sem=edge_send, recv_sem=edge_recv.at[side],
+            device_id={"yz": peer}, device_id_type=MESH,
+        )
+
+    def pass_on(side):
+        return pltpu.make_async_remote_copy(
+            src_ref=part(recv, (NYZ - 1) * (1 - side), 0, BX), dst_ref=part(recv, LOW + side, 0, BX),
+            send_sem=pass_send.at[side], recv_sem=pass_recv.at[side],
+            device_id=ids["y-" if side else "y+"], device_id_type=MESH,
+        )
+
+    mine = pl.ds(me * TILE, TILE)
+    recv[mine, :] = sendbuf[mine, :]
+    partners(send_part(0, 0, FACE))
+    pl.when(last)(lambda: partners(lambda peer: edge_tile(peer, 0).start()))
+    pl.when(first)(lambda: partners(lambda peer: edge_tile(peer, 1).start()))
+
+    pl.when(behind)(pack_first)
     send_lanes(0, l0, lambda s: packs[s])
     start(0, l0, ("x+", "x-"))
     send_rows(0, l0)
-    pl.when(jnp.logical_not(special))(lambda: partners(send_part(1, FACE, TILE - FACE)))
-
-    for load in loads[3:]:
-        load.wait()
-
-    @pl.loop(0, SPECIES)
-    def _(s):
-        charge_of = quarter_valence(s)
-        for x in range(BX):
-            for y in range(0, BY, HALF):
-                rows = slice(x * BY + y, x * BY + y + HALF)
-                centre, spread, diff = differences(l0, s, x, y)
-                diffusion = dif[s, rows, :]
-                scaled = charge_of * diffusion
-                total = centre + diffusion * spread
-                for axis in range(3):
-                    total = total + (0.5 * vel[axis, rows, :]) * diff[axis]
-                    grad[axis, s, rows, :] = scaled * diff[axis]
-                base[s, rows, :] = total
-
+    pl.when(jnp.logical_not(special) & ahead)(lambda: partners(send_part(1, FACE, TILE - FACE)))
+
+    @pl.when(behind)
+    def _():
+        load_rest()
+        first_own(0, SPECIES)
+
+    pl.when(jnp.logical_not(special) & behind)(lambda: partners(send_part(1, FACE, TILE - FACE)))
+
+    bytes_of(recv, (NYZ - 1) * FACE, a2a_recv.at[0]).wait()
+
+    def assemble(x):
+        pot[0, padded_row(x) : padded_row(x) + BY, :] = recv[pl.ds(PLACE[x], BY, stride=TILE), :]
+
+    assemble(0)
+    assemble(BX - 1)
+    start(STEPS, pot, ("x+", "x-"))
     pl.when(jnp.logical_not(last))(lambda: edge_tile(lax.rem(me + 1, NYZ), 0).wait_recv())
     pl.when(jnp.logical_not(first))(lambda: edge_tile(lax.rem(me + 1, NYZ), 1).wait_recv())
     pl.when(has["y+"])(lambda: pass_on(0).start())
     pl.when(has["y-"])(lambda: pass_on(1).start())
-    arrived(0, FACE)
-
-    def assemble(x):
-        pot[0, padded_row(x) : padded_row(x) + BY, :] = recv[pl.ds(PLACE[x], BY, stride=TILE), :]
-
-    assemble(0)
-    assemble(BX - 1)
-    start(STEPS, pot, ("x+", "x-"))
 
     def rim_terms(axis, side, s, rows):
         diffusion, flow = dif[s, rows, :], 0.5 * vel[axis, rows, :]
@@ -430,27 +431,25 @@
             to_base, to_grad = rim_terms(1, side, s, rows)
             base[s, rows, :] += to_base * value
             grad[1, s, rows, :] += to_grad * value
-        for x in range(BX):
-            rows = slice(x * BY, (x + 1) * BY)
-            value = unpack_plane(came[s], x)
+        for x, r in EVERY:
+            rows = slice(x * BY + 8 * r, x * BY + 8 * r + 8)
+            value = unpack(came[s], x, r)
             diffusion, flow = dif[s, rows, :], 0.5 * vel[2, rows, :]
             scaled = quarter_valence(s) * diffusion
-            base[s, rows, :] += (diffusion + jnp.where(at_low, -flow, flow)) * value
-            grad[2, s, rows, :] += jnp.where(at_low, -scaled, scaled) * value
-
-    arrived(1, TILE - FACE)
+            base[s, rows, :] += (diffusion + jnp.where(tile_low, -flow, flow)) * value
+            grad[2, s, rows, :] += jnp.where(tile_low, -scaled, scaled) * value
+
+    pl.when(special)(
+        lambda: bytes_of(recv, (NYZ - 2) * (TILE - FACE), a2a_recv.at[1]).wait()
+    )
+    pl.when(jnp.logical_not(special))(
+        lambda: bytes_of(recv, (NYZ - 3) * (TILE - FACE), a2a_recv.at[1]).wait()
+    )
     for x in range(1, BX - 1):
         assemble(x)
-    pl.when(has["y-"])(lambda: pass_on(0).wait_recv())
-    pl.when(has["y+"])(lambda: pass_on(1).wait_recv())
-    for side, row in ((0, padded_row(0) - 1), (1, padded_row(0) + BY)):
-        at = (LOW + side) * TILE
-        pot[0, pl.ds(row, BX - 1, stride=ROWS), :] = recv[at + 1 : at + BX, :]
-        row += (BX - 1) * ROWS
-        pot[0, row : row + 1, :] = recv[at : at + 1, :]
     z_rims = pltpu.roll(recv[pl.ds(BX, BY, stride=TILE), :], (BZ - p) & (BZ - 1), 1)
 
-    def first_step(x, packed):
+    def first_step(x):
         rims_here = pltpu.roll(z_rims, BZ - 16 * x, 1) if x else z_rims
         for y in range(0, BY, HALF):
             r = padded_row(x) + y
@@ -471,17 +470,36 @@
                 for axis in range(3):
                     total = total - here[axis] * grad[axis, s, rows, :]
                 l1[s, r : r + HALF, :] = total
-        return [merge(packed[s], own_plane(l1, s, x), x) for s in range(SPECIES)]
-
-    packed = [line] * SPECIES
-    for x in range(1, BX - 1):
-        packed = first_step(x, packed)
+
+    for x in range(BX):
+        first_step(x)
+    packed = [pack(line, own_tiles(l1, s), INNER) for s in range(SPECIES)]
+    pl.when(has["y-"])(lambda: pass_on(0).wait_recv())
+    pl.when(has["y+"])(lambda: pass_on(1).wait_recv())
+    for side in (0, 1):
+        at = (LOW + side) * TILE
+        change = pltpu.roll(recv[at : at + BX, :], BX - 1, 0)
+        change = change if side else -change
+        rows = pl.ds((BY - 1) * side, BX, stride=BY)
+        padded_rows = pl.ds(padded_row(0) + (BY - 1) * side, BX, stride=ROWS)
+        slope[1, rows, :] += change
+        for s in range(SPECIES):
+            l1[s, padded_rows, :] -= change * grad[1, s, rows, :]
+    packed = [pack(packed[s], own_tiles(l1, s), EDGES) for s in range(SPECIES)]
     receive(STEPS, pot, ("x+", "x-"))
-    for x in (0, BX - 1):
-        packed = first_step(x, packed)
+    for side in (0, 1):
+        x = (BX - 1) * side
+        change = -pot_in[side, 0] if side else pot_in[side, 0]
+        rows = slice(x * BY, (x + 1) * BY)
+        for s in range(SPECIES):
+            l1[s, padded_row(x) : padded_row(x) + BY, :] += change * grad[0, s, rows, :]
+    start(1, l1, ("x+", "x-"))
+    packed = [pack(packed[s], own_tiles(l1, s), FACES) for s in range(SPECIES)]
     send_lanes(1, l1, lambda s: packed[s])
-    start(1, l1, ("x+", "x-"))
     send_rows(1, l1)
+    for side in (0, 1):
+        rows = slice((BX - 1) * side * BY, ((BX - 1) * side + 1) * BY)
+        slope[0, rows, :] += pot_in[side, 0] if side else -pot_in[side, 0]
 
     def own_values(step, now, later, row_of):
         @pl.loop(0, SPECIES)
@@ -504,76 +522,84 @@
                     r = row_of(x) + y
                     later[s, r : r + HALF, :] = total
 
-    def outer_values(step, later, row_of):
-        apart = row_of(1) - row_of(0)
-
-        @pl.loop(0, SPECIES)
-        def _(s):
+    def x_values(step, later, row_of):
+        for s in range(SPECIES):
             for side in (0, 1):
                 x = (BX - 1) * side
                 rows = slice(x * BY, (x + 1) * BY)
                 rate = along[0, s, rows, :]
                 factor = dif[s, rows, :] + (rate if side else -rate)
                 later[s, row_of(x) : row_of(x) + BY, :] += factor * x_in[step, side, s]
+
+    def y_values(step, later, row_of):
+        apart = row_of(1) - row_of(0)
+        for s in range(SPECIES):
+            for side in (0, 1):
                 rows = pl.ds((BY - 1) * side, BX, stride=BY)
                 rate = along[1, s, rows, :]
                 factor = dif[s, rows, :] + (rate if side else -rate)
                 later[s, pl.ds(row_of(0) + (BY - 1) * side, BX, stride=apart), :] += factor * y_in[step, side, s]
 
-    def lane_factor(s, x):
-        rows = slice(x * BY, (x + 1) * BY)
-        rate = along[2, s, rows, :]
-        return dif[s, rows, :] + jnp.where(at_low, -rate, rate)
-
-    def lane_values(s, planes, later, row_of):
-        for x in planes:
-            later[s, row_of(x) : row_of(x) + BY, :] += lane_factor(s, x) * unpack_plane(came[s], x)
+    def lane_factor(s):
+        def tile_of(x, r):
+            rows = slice(x * BY + 8 * r, x * BY + 8 * r + 8)
+            rate = along[2, s, rows, :]
+            return dif[s, rows, :] + jnp.where(tile_low, -rate, rate)
+        return tile_of
+
+    def lane_values(s, places, later, row_of):
+        factor = lane_factor(s)
+        for x, r in places:
+            row = row_of(x) + 8 * r
+            later[s, row : row + 8, :] += factor(x, r) * unpack(came[s], x, r)
+
+    def by_pairs(act):
+        @pl.loop(0, SPECIES // 2)
+        def _(pair):
+            act(2 * pair)
+            act(2 * pair + 1)
 
     own_values(1, l1, l2, padded_row)
 
-    @pl.loop(0, SPECIES)
-    def _(s):
-        factors[s] = packed_rims(lambda x: lane_factor(s, x))
-
-    receive(1, l1, ("y+", "y-", "x+", "x-"))
-    outer_values(1, l2, padded_row)
-
-    @pl.loop(0, SPECIES)
-    def _(s):
-        packs[s] = packed_rims(lambda x: own_plane(l2, s, x))
-
+    def pack_factors(s):
+        factors[s] = pack(line, lane_factor(s), EVERY)
+
+    by_pairs(pack_factors)
+    packed = [pack(line, own_tiles(l2, s), INNER) for s in range(SPECIES)]
+    receive(1, l1, ("y+", "y-"))
+    y_values(1, l2, padded_row)
+    packed = [pack(packed[s], own_tiles(l2, s), EDGES) for s in range(SPECIES)]
+    receive(1, l1, ("x+", "x-"))
+    x_values(1, l2, padded_row)
+    packed = [pack(packed[s], own_tiles(l2, s), FACES) for s in range(SPECIES)]
     receive_lanes(1, l1)
-    send_lanes(2, l2, lambda s: packs[s] + factors[s] * came[s])
-
-    @pl.loop(0, SPECIES)
-    def _(s):
-        lane_values(s, (0, BX - 1), l2, padded_row)
-
+    send_lanes(2, l2, lambda s: packed[s] + factors[s] * came[s])
+    for s in range(SPECIES):
+        lane_values(s, FACES, l2, padded_row)
     start(2, l2, ("x+", "x-"))
-
-    @pl.loop(0, SPECIES)
-    def _(s):
-        lane_values(s, range(1, BX - 1), l2, padded_row)
-
+    for s in range(SPECIES):
+        lane_values(s, EDGES, l2, padded_row)
     send_rows(2, l2)
+    by_pairs(lambda s: lane_values(s, INNER, l2, padded_row))
 
     flat_row = lambda x: x * BY
     own_values(2, l2, l3, flat_row)
-    receive(2, l2, ("y+", "y-", "x+", "x-"))
-    outer_values(2, l3, flat_row)
+    receive(2, l2, ("y+", "y-"))
+    y_values(2, l3, flat_row)
     receive_lanes(2, l2)
 
-    @pl.loop(0, SPECIES)
-    def _(s):
-        lane_values(s, range(BX), l3, flat_row)
+    by_pairs(lambda s: lane_values(s, EVERY, l3, flat_row))
+    receive(2, l2, ("x+", "x-"))
+    x_values(2, l3, flat_row)
 
     @pl.when(special)
     def _():
-        bytes_of(sendbuf, (NYZ - 1) * TILE, edge_send).wait()
+        bytes_of(sendbuf, (NYZ - 1) * (TILE - FACE), edge_send).wait()
+
+    bytes_of(sendbuf, (NYZ - 1) * FACE, a2a_send.at[0]).wait()
 
     @pl.when(jnp.logical_not(special))
     def _():
-        bytes_of(sendbuf, (NYZ - 1) * FACE, a2a_send.at[0]).wait()
         bytes_of(sendbuf, (NYZ - 1) * (TILE - FACE), a2a_send.at[1]).wait()
 
     pl.when(has["y+"])(lambda: pass_on(0).wait_send())
@@ -624,6 +650,7 @@
             pltpu.VMEM((STEPS, 2, SPECIES, BX, BZ), F32),
             pltpu.VMEM((STEPS, 2, SPECIES // 2, 8, BZ), F32),
             pltpu.VMEM((STEPS, 2, SPECIES // 2, 8, BZ), F32),
+            pltpu.VMEM((2, 1, BY, BZ), F32),
             pltpu.VMEM((SPECIES, 8, BZ), F32),
             pltpu.VMEM((SPECIES, 8, BZ), F32),
             pltpu.VMEM((SPECIES, 8, BZ), F32),

time: 36.8 us -> 35.5 us (0.965)
  Pallas kernels: 35.8 us -> 34.4 us
    pallas_call x1, Pallas kernels: 35.8 us -> 34.4 us  [body(): pl.pallas_call(slab_kernel, out_shape=pltpu.VMEM(brick, F32), in_specs=[a...]
where the time goes in v4:
time: 35.5 us; the launch traced here: 35.4 us
  Pallas kernels  34.4 us (97%)
  local copies, waits for them, and re-layouts  0.97 us (3%)
    pallas_call x1, Pallas kernels, body(): pl.pallas_call(slab_kernel, out_shape=pltpu.VMEM(brick, F32), in_specs=[a...  34.4 us
    unnamed x1, local copies, waits for them, and re-layouts  0.97 us

profile of v4, /device:TPU:1, one launch (start us, length us, event | category | flops | bytes accessed | tf_op | source)
XLA Modules:
  0.0 35.4 jit_solution(4810602923815708065)
XLA Ops:
  0.0 34.4 %shard_map.64 = f32[4,512,128]{2,1,0:T(8,128)S(1)} custom-call(f32[4,8,64,128]{3,2,1,0:T(8,128)} %bitcast.8, f32[4,512,128]{2,1,0:T(8,128)} %bitcast.9, f32[3,512,128]{2,1,0:T(8,128)} %bitcast.10, f32[8,16,512]{2,1,0:T(8,128)} %bitcast.11, bf16[512,128]{1,0:T(8,128)(2,1)} %constant.4.clone.high_hbm, bf16[512,128]{1,0:T(8,128)(2,1)} %constant.5.clone.low_hbm), custom_call_target="tpu_custom_call" | custom-call | tf_op jit(solution)/shard_map/pallas_call | solution.py:629
  34.4 1.0 %copy.9 = f32[4,8,64,1,128]{4,3,2,1,0:T(1,128)} copy(f32[4,8,64,1,128]{4,3,2,1,0:T(1,128)S(1)} %bitcast.7) | data formatting | bytes 2097152

commit v5 on v4

--- a/solution.py
+++ b/solution.py
@@ -92,8 +92,8 @@
 def slab_kernel(
     lam_hbm, dif_hbm, vel_hbm, cm_hbm, high_hbm, low_hbm, l3,
     l0, l1, l2, dif, vel, along, base, grad, slope, pot, cm, high, low,
-    product, sendbuf, recv, x_in, y_out, y_in, z_out, z_in, pot_in, packs, factors, came,
-    load_sem, lam_sem, a2a_send, a2a_recv, edge_send, edge_recv, pass_send, pass_recv, halo_send, halo_recv,
+    product, sendbuf, recv, x_in, y_out, y_in, z_out, z_in, pot_in, side_out, side_in, packs, factors, x_factors, came,
+    load_sem, lam_sem, a2a_send, a2a_recv, edge_send, edge_recv, pass_send, pass_recv, group_in, far_send, far_recv, halo_send, halo_recv,
 ):
     gx = lax.axis_index("gx")
     me = lax.axis_index("yz")
@@ -111,8 +111,14 @@
         "y+": {"yz": me + 1}, "y-": {"yz": me - 1},
         "z+": {"yz": me + PY}, "z-": {"yz": me - PY},
     }
+    lower, upper = gx == 1, gx == 2
+    far_gx = jnp.where(lower, 2, 1)
+    middle = lower | upper
+    for way in "+-":
+        has["l" + way], ids["l" + way] = has["x" + way], ids["x" + way]
     ways = ("z+", "z-", "x+", "x-", "y+", "y-")
-    back = {"x+": "x-", "x-": "x+", "y+": "y-", "y-": "y+", "z+": "z-", "z-": "z+"}
+    numbers = ways + ("l+", "l-")
+    back = {"x+": "x-", "x-": "x+", "y+": "y-", "y-": "y+", "z+": "z-", "z-": "z+", "l+": "l-", "l-": "l+"}
 
     def partners(act):
         @pl.loop(0, 8)
@@ -129,17 +135,6 @@
                     else:
                         pl.when(j < 7)(functools.partial(act, peer))
 
-    barrier = pltpu.get_barrier_semaphore()
-    partners(
-        lambda peer: pl.semaphore_signal(
-            barrier, inc=1, device_id={"yz": peer}, device_id_type=MESH
-        )
-    )
-    for way in ("x+", "x-"):
-        @pl.when(has[way])
-        def _():
-            pl.semaphore_signal(barrier, inc=1, device_id=ids[way], device_id_type=MESH)
-
     loads = [
         pltpu.make_async_copy(cm_hbm, cm, load_sem.at[0]),
         pltpu.make_async_copy(high_hbm, high, load_sem.at[1]),
@@ -151,7 +146,21 @@
         pltpu.make_async_copy(lam_hbm.at[:, x], l0.at[:, pl.ds(padded_row(x), BY), :], lam_sem.at[x])
         for x in range(BX)
     ]
-    for load in loads[:3] + lam_loads + loads[3:]:
+    for load in loads[:3]:
+        load.start()
+
+    barrier = pltpu.get_barrier_semaphore()
+    partners(
+        lambda peer: pl.semaphore_signal(
+            barrier, inc=1, device_id={"yz": peer}, device_id_type=MESH
+        )
+    )
+    for way in ("x+", "x-"):
+        @pl.when(has[way])
+        def _():
+            pl.semaphore_signal(barrier, inc=1, device_id=ids[way], device_id_type=MESH)
+
+    for load in lam_loads + loads[3:]:
         load.start()
 
     zero = jnp.zeros((BY, BZ), F32)
@@ -176,6 +185,8 @@
                 for s in range(SPECIES):
                     x_in[stage, side, s] = zero
             pot_in[side, 0] = zero
+            for s in range(SPECIES):
+                side_in[side, s] = line
 
         @pl.when(jnp.logical_not(has["y" + way]))
         def _():
@@ -224,7 +235,7 @@
             sendbuf[at : at + 1, :] = rows[q % 2]
 
     def halo_copy(stage, way, fields):
-        number = ways.index(way)
+        number = numbers.index(way)
         side = 0 if way[1] == "+" else 1
         if way[0] == "x":
             src = fields.at[:, pl.ds(padded_row(BX - 1 if side == 0 else 0), BY), :]
@@ -232,6 +243,8 @@
                 dst = pot_in.at[side]
             else:
                 dst = x_in.at[stage, side]
+        elif way[0] == "l":
+            src, dst = side_out, side_in.at[side]
         elif way[0] == "y":
             src, dst = y_out.at[stage, side], y_in.at[stage, side]
         else:
@@ -342,6 +355,10 @@
         NYZ - 1 + has["x+"].astype(jnp.int32) + has["x-"].astype(jnp.int32),
     )
 
+    @pl.when(middle)
+    def _():
+        pl.semaphore_signal(group_in, inc=1, device_id={"gx": far_gx}, device_id_type=MESH)
+
     def part(ref, index, start, count):
         return ref.at[pl.ds(index * TILE + start, count), :]
 
@@ -385,6 +402,27 @@
     send_lanes(0, l0, lambda s: packs[s])
     start(0, l0, ("x+", "x-"))
     send_rows(0, l0)
+    def far_row(side):
+        def act(peer):
+            pltpu.make_async_remote_copy(
+                src_ref=part(sendbuf, peer, PLACE[0 if side else BX - 1], 1),
+                dst_ref=pot_in.at[side, 0, pl.ds(me, 1), :],
+                send_sem=far_send, recv_sem=far_recv,
+                device_id={"gx": far_gx, "yz": peer}, device_id_type=MESH,
+            ).start()
+        return act
+
+    def send_far(side):
+        partners(far_row(side))
+        far_row(side)(me)
+
+    @pl.when(middle)
+    def _():
+        pl.semaphore_wait(group_in, 1)
+
+    pl.when(lower)(lambda: send_far(0))
+    pl.when(upper)(lambda: send_far(1))
+
     pl.when(jnp.logical_not(special) & ahead)(lambda: partners(send_part(1, FACE, TILE - FACE)))
 
     @pl.when(behind)
@@ -401,7 +439,8 @@
 
     assemble(0)
     assemble(BX - 1)
-    start(STEPS, pot, ("x+", "x-"))
+    pl.when(jnp.logical_not(lower))(lambda: start(STEPS, pot, ("x+",)))
+    pl.when(jnp.logical_not(upper))(lambda: start(STEPS, pot, ("x-",)))
     pl.when(jnp.logical_not(last))(lambda: edge_tile(lax.rem(me + 1, NYZ), 0).wait_recv())
     pl.when(jnp.logical_not(first))(lambda: edge_tile(lax.rem(me + 1, NYZ), 1).wait_recv())
     pl.when(has["y+"])(lambda: pass_on(0).start())
@@ -486,16 +525,21 @@
         for s in range(SPECIES):
             l1[s, padded_rows, :] -= change * grad[1, s, rows, :]
     packed = [pack(packed[s], own_tiles(l1, s), EDGES) for s in range(SPECIES)]
-    receive(STEPS, pot, ("x+", "x-"))
+    pl.when(jnp.logical_not(upper))(lambda: receive(STEPS, pot, ("x+",)))
+    pl.when(jnp.logical_not(lower))(lambda: receive(STEPS, pot, ("x-",)))
+    pl.when(middle)(lambda: bytes_of(sendbuf, BY, far_recv).wait())
     for side in (0, 1):
         x = (BX - 1) * side
         change = -pot_in[side, 0] if side else pot_in[side, 0]
         rows = slice(x * BY, (x + 1) * BY)
         for s in range(SPECIES):
             l1[s, padded_row(x) : padded_row(x) + BY, :] += change * grad[0, s, rows, :]
-    start(1, l1, ("x+", "x-"))
     packed = [pack(packed[s], own_tiles(l1, s), FACES) for s in range(SPECIES)]
     send_lanes(1, l1, lambda s: packed[s])
+    for s in range(SPECIES):
+        side_out[s] = packed[s]
+    start(1, l1, ("l+", "l-"))
+    start(1, l1, ("x+", "x-"))
     send_rows(1, l1)
     for side in (0, 1):
         rows = slice((BX - 1) * side * BY, ((BX - 1) * side + 1) * BY)
@@ -564,16 +608,30 @@
     def pack_factors(s):
         factors[s] = pack(line, lane_factor(s), EVERY)
 
+        def x_factor(x, r):
+            rows = slice(x * BY + 8 * r, x * BY + 8 * r + 8)
+            rate = along[0, s, rows, :]
+            return dif[s, rows, :] + (rate if x else -rate)
+
+        x_factors[s] = pack(line, x_factor, FACES)
+
     by_pairs(pack_factors)
     packed = [pack(line, own_tiles(l2, s), INNER) for s in range(SPECIES)]
     receive(1, l1, ("y+", "y-"))
     y_values(1, l2, padded_row)
-    packed = [pack(packed[s], own_tiles(l2, s), EDGES) for s in range(SPECIES)]
+    packed = [pack(packed[s], own_tiles(l2, s), OUTER) for s in range(SPECIES)]
+    receive(1, l1, ("l+", "l-"))
+    slab = ((lanes() + 1) >> 4) & (BX - 1)
+
+    def beside(s):
+        low, high = pltpu.roll(side_in[0, s], 16, 1), pltpu.roll(side_in[1, s], BZ - 16, 1)
+        return jnp.where(slab == 0, low, jnp.where(slab == BX - 1, high, 0.0))
+
+    packed = [packed[s] + x_factors[s] * beside(s) for s in range(SPECIES)]
+    receive_lanes(1, l1)
+    send_lanes(2, l2, lambda s: packed[s] + factors[s] * came[s])
     receive(1, l1, ("x+", "x-"))
     x_values(1, l2, padded_row)
-    packed = [pack(packed[s], own_tiles(l2, s), FACES) for s in range(SPECIES)]
-    receive_lanes(1, l1)
-    send_lanes(2, l2, lambda s: packed[s] + factors[s] * came[s])
     for s in range(SPECIES):
         lane_values(s, FACES, l2, padded_row)
     start(2, l2, ("x+", "x-"))
@@ -606,7 +664,10 @@
     pl.when(has["y-"])(lambda: pass_on(1).wait_send())
     for stage, ref in enumerate((l0, l1, l2)):
         finish(stage, ref)
-    finish(STEPS, pot, ("x+", "x-"))
+    finish(1, l1, ("l+", "l-"))
+    pl.when(jnp.logical_not(lower))(lambda: finish(STEPS, pot, ("x+",)))
+    pl.when(jnp.logical_not(upper))(lambda: finish(STEPS, pot, ("x-",)))
+    pl.when(middle)(lambda: bytes_of(sendbuf, BY, far_send).wait())
 
 
 def hand_over_kernel(source, target, sems):
@@ -652,6 +713,9 @@
             pltpu.VMEM((STEPS, 2, SPECIES // 2, 8, BZ), F32),
             pltpu.VMEM((2, 1, BY, BZ), F32),
             pltpu.VMEM((SPECIES, 8, BZ), F32),
+            pltpu.VMEM((2, SPECIES, 8, BZ), F32),
+            pltpu.VMEM((SPECIES, 8, BZ), F32),
+            pltpu.VMEM((SPECIES, 8, BZ), F32),
             pltpu.VMEM((SPECIES, 8, BZ), F32),
             pltpu.VMEM((SPECIES, 8, BZ), F32),
             pltpu.SemaphoreType.DMA((5,)),
@@ -662,8 +726,11 @@
             pltpu.SemaphoreType.DMA((2,)),
             pltpu.SemaphoreType.DMA((2,)),
             pltpu.SemaphoreType.DMA((2,)),
-            pltpu.SemaphoreType.DMA((STEPS + 1, 6)),
-            pltpu.SemaphoreType.DMA((STEPS + 1, 6)),
+            pltpu.SemaphoreType.REGULAR,
+            pltpu.SemaphoreType.DMA,
+            pltpu.SemaphoreType.DMA,
+            pltpu.SemaphoreType.DMA((STEPS + 1, 8)),
+            pltpu.SemaphoreType.DMA((STEPS + 1, 8)),
         ],
         compiler_params=pltpu.CompilerParams(
             collective_id=0, has_side_effects=True, vmem_limit_bytes=60 * 1024 * 1024

time: 35.5 us -> 35.6 us (level)
  no operation moved by 1% of the time
where the time goes in v5:
time: 35.6 us; the launch traced here: 35.5 us
  Pallas kernels  34.5 us (97%)
  local copies, waits for them, and re-layouts  0.97 us (3%)
    pallas_call x1, Pallas kernels, body(): pl.pallas_call(slab_kernel, out_shape=pltpu.VMEM(brick, F32), in_specs=[a...  34.5 us
    unnamed x1, local copies, waits for them, and re-layouts  0.97 us

profile of v5, /device:TPU:1, one launch (start us, length us, event | category | flops | bytes accessed | tf_op | source)
XLA Modules:
  0.0 35.5 jit_solution(605429875422740900)
XLA Ops:
  0.0 34.5 %shard_map.64 = f32[4,512,128]{2,1,0:T(8,128)S(1)} custom-call(f32[4,8,64,128]{3,2,1,0:T(8,128)} %bitcast.8, f32[4,512,128]{2,1,0:T(8,128)} %bitcast.9, f32[3,512,128]{2,1,0:T(8,128)} %bitcast.10, f32[8,16,512]{2,1,0:T(8,128)} %bitcast.11, bf16[512,128]{1,0:T(8,128)(2,1)} %constant.4.clone.high_hbm, bf16[512,128]{1,0:T(8,128)(2,1)} %constant.5.clone.low_hbm), custom_call_target="tpu_custom_call" | custom-call | tf_op jit(solution)/shard_map/pallas_call | solution.py:690
  34.6 1.0 %copy.9 = f32[4,8,64,1,128]{4,3,2,1,0:T(1,128)} copy(f32[4,8,64,1,128]{4,3,2,1,0:T(1,128)S(1)} %bitcast.7) | data formatting | bytes 2097152
